TPU v7x, 32 devices: a whole 2x2x4 slice. The times are simulated.
32 devices in a mesh: groups: 2 (over y), vis: 8 (over z, x), band: 2 (over core).
Axes of the slice: x: 2, y: 2, z: 4, core: 2. Of those that a mesh axis runs over, the one named last changes fastest.
Arguments:
- pieces: bfloat16 [2, 3072, 128, 128], P('band', ('groups', 'vis')), parts along dimension 1, may hold values from -6 to 6
- visit: int32 [2, 3072], P('band', ('groups', 'vis')), parts along dimension 1, may hold values from 0 to 23
- tile_map: int32 [2, 3072, 1], P('band', ('groups', 'vis')), parts along dimension 1, may hold values from 0 to 7; in each aligned block of 192 rows (0 to 191, 192 to 383, ..., all dimensions but the last counted through in order) at most 48 rows name the same one
- good_columns: int32 [2, 3072, 4], P('band', ('groups', 'vis')), parts along dimension 1, may hold values from -2147483648 to 2147483646, as said below
- psf_taps: float32 [2, 3072, 2, 21], P('band', ('groups', 'vis')), parts along dimension 1, may hold values from 0.05 to 1
- shifts: float32 [2, 3072, 2], P('band', ('groups', 'vis')), parts along dimension 1, may hold values from -0.5 to 0.5
- calib: float32 [2, 24], P('band'), may hold values from 0.5 to 2
- weights: int32 [2, 24], P('band'), may hold values from 1 to 8
- band_gain: float32 [2], P('band'), may hold values from 0.5 to 2
Outputs:
- coadd: float32 [2, 2048, 128], P('band', ('groups', 'vis')), parts along dimension 1
- detection: float32 [2048, 128], P(('groups', 'vis')), parts along dimension 0
There are 2 independent parts, one for each index of `groups`. A program takes and returns all parts, laid end to end along the dimension named above; an argument that names none is the same for every part. Nothing has to cross between parts.
Inputs may be any that keep to these rules, and one draw needn't show every extreme that they name: `tile_map`: among the 192 pieces of one band on one index of vis (aligned blocks of 192 pieces), no tile appears more than 48 times, a bound that some block reaches. `good_columns`: independent random bits.
All inputs are finite; a program needn't handle non-finite values.
Results may differ from a plain program's by a relative error of at most 0.0081.
Values may be sent and summed in bfloat16 or wider, within the bound.
A program may use at most 128 MiB of HBM per device.

v0:
```python
import jax
import jax.numpy as jnp
from jax import lax
from jax.sharding import PartitionSpec as P


def good_mask(words):
    bits = jnp.arange(32, dtype=jnp.int32)
    flags = jnp.right_shift(words[..., None], bits) & 1
    return flags.reshape(words.shape[:-1] + (words.shape[-1] * 32,)).astype(jnp.float32)


def kernel_matrix(taps, size):
    kernel = taps / jnp.sum(taps, axis=-1, keepdims=True)
    count = taps.shape[-1]
    reach = (count - 1) // 2
    places = jnp.arange(size, dtype=jnp.int32)
    offset = places[None, :] - places[:, None] + reach
    table = (offset[None, :, :] == jnp.arange(count, dtype=jnp.int32)[:, None, None]).astype(
        jnp.float32
    )
    result = jnp.einsum("pt,tij->pij", kernel, table, precision=lax.Precision.HIGHEST)
    return result.astype(jnp.bfloat16)


def lanczos(values):
    inside = jnp.abs(values) < 3.0
    return jnp.where(inside, jnp.sinc(values) * jnp.sinc(values / 3.0), 0.0)


def warp_matrix(offset, size):
    places = jnp.arange(size).astype(jnp.float32)
    spread = places[None, None, :] - places[None, :, None] - offset[:, None, None]
    steps = jnp.arange(-3, 4).astype(jnp.float32)
    norms = jnp.sum(lanczos(steps[None, :] - offset[:, None]), axis=1)
    return (lanczos(spread) / norms[:, None, None]).astype(jnp.bfloat16)


def warp_pieces(pieces, visit, words, taps, shifts, calib, weights):
    size = pieces.shape[-1]
    good = good_mask(words)
    match = (visit[:, None] == jnp.arange(calib.shape[0], dtype=jnp.int32)[None, :]).astype(
        jnp.float32
    )
    scale = jnp.dot(match, calib, precision=lax.Precision.HIGHEST)
    weight = jnp.sum(match * weights.astype(jnp.float32)[None, :], axis=1)
    calibrated = (pieces.astype(jnp.float32) * scale[:, None, None] * good[:, None, :]).astype(
        jnp.bfloat16
    )
    w_rows = warp_matrix(shifts[:, 0], size)
    w_cols = warp_matrix(shifts[:, 1], size)
    k_rows = kernel_matrix(taps[:, 0], size)
    k_cols = kernel_matrix(taps[:, 1], size)
    left = jnp.einsum("pij,pjk->pik", w_rows, k_rows, preferred_element_type=jnp.float32).astype(
        jnp.bfloat16
    )
    right = jnp.einsum("pij,pjk->pik", w_cols, k_cols, preferred_element_type=jnp.float32).astype(
        jnp.bfloat16
    )
    inner = jnp.einsum(
        "pij,pkj->pik", calibrated, right, preferred_element_type=jnp.float32
    ).astype(jnp.bfloat16)
    warped = jnp.einsum("pij,pjk->pik", left, inner, preferred_element_type=jnp.float32)
    num_piece = (warped * weight[:, None, None]).astype(jnp.bfloat16)
    row_weight = (jnp.sum(left.astype(jnp.float32), axis=2) * weight[:, None]).astype(jnp.bfloat16)
    col_good = jnp.einsum("pij,pj->pi", right.astype(jnp.float32), good).astype(jnp.bfloat16)
    return (num_piece, row_weight, col_good)


def shards(pieces, visit, tile_map, good_columns, psf_taps, shifts, calib, weights, band_gain):
    num_piece, row_weight, col_good = warp_pieces(
        pieces[0], visit[0], good_columns[0], psf_taps[0], shifts[0], calib[0], weights[0]
    )
    count = num_piece.shape[0]
    size = num_piece.shape[-1]
    owners = lax.axis_size("vis")
    capacity = max(2, 2 * count // owners)
    tile = tile_map[0, :, 0]
    onehot = (tile[:, None] == jnp.arange(owners, dtype=jnp.int32)[None, :]).astype(jnp.int32)
    before = jnp.cumsum(onehot, axis=0) - onehot
    rank = jnp.sum(before * onehot, axis=1)
    slot = tile * capacity + rank
    vectors = jnp.stack([row_weight, col_good], axis=1)
    vec_buffer = jnp.zeros((owners * capacity, 2, size), jnp.bfloat16).at[slot].set(vectors)
    got_vec = lax.all_to_all(vec_buffer, "vis", split_axis=0, concat_axis=0, tiled=True)
    flat = num_piece.reshape(count, size * size)
    select = (
        tile[:, None] == jnp.arange(1 * lax.axis_size("vis"), dtype=jnp.int32)[None, :]
    ).astype(jnp.bfloat16)
    summed = jnp.einsum("pc,pk->ck", select, flat, preferred_element_type=jnp.float32)
    total = lax.psum_scatter(
        summed.reshape(1 * lax.axis_size("vis"), size, size), "vis", scatter_dimension=0, tiled=True
    )[0]
    den = jnp.dot(got_vec[:, 0, :].T, got_vec[:, 1, :], preferred_element_type=jnp.float32)
    coadd = total / jnp.maximum(den, 1.0)
    detection = lax.psum(band_gain[0] * coadd, "band")
    return (coadd[None], detection)


def solution(mesh):
    placed = (
        P("band", ("groups", "vis"), None, None),
        P("band", ("groups", "vis")),
        P("band", ("groups", "vis"), None),
        P("band", ("groups", "vis"), None),
        P("band", ("groups", "vis"), None, None),
        P("band", ("groups", "vis"), None),
        P("band", None),
        P("band", None),
        P("band"),
    )
    return jax.shard_map(
        shards,
        mesh=mesh,
        in_specs=placed,
        out_specs=(P("band", ("groups", "vis"), None), P(("groups", "vis"), None)),
        check_vma=False,
    )
```

profile of v0, /device:TPU:0, one launch (start us, length us, event | category | flops | bytes accessed | tf_op | source)
XLA Modules:
  0.0 220.6 jit_solution(6516371349511531576)
XLA Ops:
  7.2 0.0 copy-start
  7.2 0.0 reduce-scatter.2.cloned.1.call-start
  7.3 0.9 slice_reduce_fusion.2
  8.2 0.8 fusion.297
  9.0 0.1 broadcast_subtract_fusion
  9.0 0.7 convert_bitcast_fusion.2
  9.7 0.1 shift_right_arithmetic.30
  9.8 0.8 fusion.156
  10.6 0.0 copy-start.1
  10.6 0.7 copy.30
  11.3 1.3 select_reduce_fusion
  12.6 0.0 copy-done
  12.6 1.4 fusion.168
  14.0 5.4 %convolution_convert_fusion.1 = bf16[192,128,128]{2,0,1:T(8,128)(2,1)S(1)} fusion(s32[128,128]{1,0:T(8,128)S(1)} %subtract_add_fusion, f32[192,1,21]{0,1,2:T(1,128)S(1)} %get-tuple-element.10, f32[192]{0:T(256)S(1)} %get-tuple-element.4), kind=kOutput, calls=%fused_computation.173 | convolution fusion | flops 796217280 | bytes 6373888 | tf_op jit(solution)/shard_map/pt,tij->pij/dot_general | solution.py:22
  19.4 5.4 %convolution_convert_fusion = bf16[192,128,128]{2,0,1:T(8,128)(2,1)S(1)} fusion(s32[128,128]{1,0:T(8,128)S(1)} %subtract_add_fusion, f32[192,1,21]{0,1,2:T(1,128)S(1)} %get-tuple-element.11, f32[192]{0:T(256)S(1)} %get-tuple-element.5), kind=kOutput, calls=%fused_computation.172 | convolution fusion | flops 796217280 | bytes 6373888 | tf_op jit(solution)/shard_map/pt,tij->pij/dot_general | solution.py:22
  24.7 0.0 copy-done.1
  24.8 0.1 fusion.266
  24.9 43.7 %convert_reduce_fusion = (f32[192,128]{1,0:T(8,128)S(1)}, bf16[192,128,128]{1,2,0:T(8,128)(2,1)}) fusion(bf16[192,128,128]{2,0,1:T(8,128)(2,1)S(1)} %convolution_convert_fusion.1, f32[192]{0:T(256)S(1)} %get-tuple-element.6, f32[192]{0:T(256)S(1)} %bitcast.116, f32[128,128]{1,0:T(8,128)S(1)} %broadcast_subtract_fusion), kind=kOutput, calls=%fused_computation.122 | convolution fusion | flops 1044357120 | bytes 12748288 | tf_op jit(solution)/shard_map/pij,pjk->pik/dot_general | solution.py:54
  68.6 0.0 copy-start.3
  68.6 0.0 copy-start.5
  68.6 0.0 copy-start.6
  68.6 40.1 %fusion.142 = bf16[192,128,128]{2,1,0:T(8,128)(2,1)} fusion(bf16[192,128,128]{2,0,1:T(8,128)(2,1)S(1)} %convolution_convert_fusion, f32[192]{0:T(256)S(1)} %get-tuple-element.7, f32[192]{0:T(256)S(1)} %bitcast.114, f32[128,128]{1,0:T(8,128)S(1)} %broadcast_subtract_fusion), kind=kOutput, calls=%fused_computation.174 | convolution fusion | flops 1038090240 | bytes 12649984 | tf_op jit(solution)/shard_map/pij,pjk->pik/dot_general | solution.py:57
  108.7 0.0 copy-done.3
  108.7 0.0 copy-done.5
  108.7 0.0 copy-done.6
  108.7 0.0 copy-start.4
  108.7 11.9 %multiply_convert_fusion = bf16[192,128,128]{2,1,0:T(8,128)(2,1)} fusion(f32[192]{0:T(256)S(1)} %copy-done.5, bf16[192,128,128]{1,2,0:T(8,128)(2,1)} %get-tuple-element.15, bf16[192,128,128]{2,1,0:T(8,128)(2,1)} %fusion.142, bf16[1,192,128,128]{3,2,1,0:T(8,128)(2,1)} %param.11, f32[192,128]{1,0:T(8,128)S(1)} %copy-done.3, f32[192]{0:T(256)S(1)} %bitcast.122), kind=kOutput, calls=%fused_computation.123 | convolution fusion | flops 1632632832 | bytes 25265664 | tf_op jit(solution)/shard_map/pij,pjk->pik/dot_general | solution.py:63
  120.6 0.0 copy-start.2
  120.6 0.0 copy-done.4
  120.6 6.2 %fusion.96 = f32[8,128,128]{2,0,1:T(8,128)S(1)} fusion(s32[192]{0:T(256)S(1)} %bitcast.107, bf16[24,8,128,128]{3,2,1,0:T(8,128)(2,1)} %bitcast.120), kind=kOutput, calls=%fused_computation.130 | convolution fusion | flops 50333184 | bytes 6816512 | tf_op jit(solution)/shard_map/pc,pk->ck/dot_general | solution.py:90
  126.8 0.9 copy.34
  127.7 0.0 reduce-scatter.2.cloned.1.call-update
  127.7 0.1 fusion.161
  127.8 0.0 copy-done.2
  127.8 0.1 copy.37
  128.0 6.1 %fusion.298 = f32[192,1,128]{2,1,0:T(1,128)S(1)} fusion(bf16[192,128,128]{2,1,0:T(8,128)(2,1)} %fusion.142, bf16[192,128,1]{1,2,0:T(2,128)(2,1)S(1)} %copy.37), kind=kOutput, calls=%fused_computation.373 | convolution fusion | flops 6291456 | bytes 6438912 | tf_op jit(solution)/shard_map/pij,pj->pi/dot_general | solution.py:66
  134.2 0.1 copy.35
  134.3 0.6 reduce-window.6
  134.9 0.2 slice_reduce_fusion
  135.1 0.1 add_bitcast_fusion
  135.2 0.8 broadcast_in_dim.22
  136.0 21.0 %scatter_fusion = bf16[384,2,128]{2,1,0:T(2,128)(2,1)} fusion(bf16[384,2,128]{2,1,0:T(2,128)(2,1)} %broadcast_in_dim.22, s32[192]{0:T(256)S(1)} %bitcast.110, bf16[192,2,128]{2,1,0:T(2,128)(2,1)S(1)} %copy.35), kind=kCustom, calls=%fused_computation | custom fusion | bytes 295680 | tf_op jit(solution)/shard_map/scatter | solution.py:84
  157.0 7.1 %all-to-all-start = ((bf16[384,2,128]{2,1,0:T(2,128)(2,1)}), bf16[384,2,128]{2,1,0:T(2,128)(2,1)S(1)}, u32[]{:S(2)}, u32[]{:S(2)}) async-start(bf16[384,2,128]{2,1,0:T(2,128)(2,1)} %scatter_fusion), calls=%async_computation.1 | async-start | bytes 393216 | tf_op jit(solution)/shard_map/all_to_all | solution.py:85
  164.0 0.0 all-reduce.3.cloned.1.call-start
  164.7 7.3 %all-to-all-done = bf16[384,2,128]{2,1,0:T(2,128)(2,1)S(1)} async-done(((bf16[384,2,128]{2,1,0:T(2,128)(2,1)}), bf16[384,2,128]{2,1,0:T(2,128)(2,1)S(1)}, u32[]{:S(2)}, u32[]{:S(2)}) %all-to-all-start) | async-done | bytes 196640 | tf_op jit(solution)/shard_map/all_to_all | solution.py:85
  172.0 0.3 fusion.296
  172.3 20.3 %reduce-scatter.2.cloned.1.call-done = f32[1,128,128]{2,1,0:T(8,128)} async-done(((f32[8,128,128]{2,1,0:T(8,128)}), f32[1,128,128]{2,1,0:T(8,128)}) %reduce-scatter.2.cloned.1.call-update) | async-done | bytes 65552 | tf_op jit(solution)/shard_map/reduce_scatter | solution.py:91
  192.6 1.7 broadcast_multiply_fusion
  194.3 0.0 all-reduce.3.cloned.1.call-update
  194.3 18.0 %all-reduce.3.cloned.1.call-done = f32[128,128]{1,0:T(8,128)} async-done(((f32[128,128]{1,0:T(8,128)}), f32[128,128]{1,0:T(8,128)}) %all-reduce.3.cloned.1.call-update) | async-done | bytes 65552 | tf_op jit(solution)/shard_map/psum | solution.py:96
  212.3 1.5 copy.85
  (12 shorter events, 0.2 us)
Async XLA Ops:
  7.2 5.5 %copy-start = (f32[1,24]{1,0:T(1,128)S(1)}, f32[1,24]{1,0:T(1,128)}, u32[]{:S(2)}) copy-start(f32[1,24]{1,0:T(1,128)} %param.17) | copy-start | bytes 292
  7.2 185.4 %reduce-scatter.2.cloned.1.call-start = ((), (), s32[]{:S(2)}) async-start(), calls=%async_computation.2 | async-start | bytes 589824 | tf_op jit(solution)/shard_map/reduce_scatter | solution.py:91
  10.6 14.2 %copy-start.1 = (f32[192,128]{0,1:T(8,128)}, f32[192,128]{0,1:T(8,128)S(1)}, u32[]{:S(2)}) copy-start(f32[192,128]{0,1:T(8,128)S(1)} %fusion.156) | copy-start | bytes 294916
  68.6 40.1 %copy-start.3 = (f32[192,128]{1,0:T(8,128)S(1)}, f32[192,128]{1,0:T(8,128)}, u32[]{:S(2)}) copy-start(f32[192,128]{1,0:T(8,128)} %copy.30) | copy-start | bytes 294916
  68.6 40.1 %copy-start.5 = (f32[192]{0:T(256)S(1)}, f32[192]{0:T(256)}, u32[]{:S(2)}) copy-start(f32[192]{0:T(256)} %select_reduce_fusion) | copy-start | bytes 2308
  68.6 40.1 %copy-start.6 = (f32[1,192]{1,0:T(1,128)S(1)}, f32[1,192]{1,0:T(1,128)}, u32[]{:S(2)}) copy-start(f32[1,192]{1,0:T(1,128)} %fusion.168) | copy-start | bytes 2308
  108.7 11.9 %copy-start.4 = (s32[1,192,1]{1,2,0:T(1,128)S(1)}, s32[1,192,1]{1,2,0:T(1,128)}, u32[]{:S(2)}) copy-start(s32[1,192,1]{1,2,0:T(1,128)} %param.13) | copy-start | bytes 2308
  120.6 7.2 %copy-start.2 = (f32[192,128]{0,1:T(8,128)S(1)}, f32[192,128]{0,1:T(8,128)}, u32[]{:S(2)}) copy-start(f32[192,128]{0,1:T(8,128)} %copy-done.1) | copy-start | bytes 294916
  157.0 15.0 %all-to-all-start = ((bf16[384,2,128]{2,1,0:T(2,128)(2,1)}), bf16[384,2,128]{2,1,0:T(2,128)(2,1)S(1)}, u32[]{:S(2)}, u32[]{:S(2)}) async-start(bf16[384,2,128]{2,1,0:T(2,128)(2,1)} %scatter_fusion), calls=%async_computation.1 | async-start | bytes 393216 | tf_op jit(solution)/shard_map/all_to_all | solution.py:85
  164.0 48.3 %all-reduce.3.cloned.1.call-start = ((), (), s32[]{:S(2)}) async-start(), calls=%async_computation.3 | async-start | bytes 131072 | tf_op jit(solution)/shard_map/psum | solution.py:96
Sparse Core Ops, SparseCore 0:
  127.8 64.6 reduce-scatter.1
  195.5 16.7 all-reduce.2
where the time goes:
time: 221 us
  matrix products  122 us (55%)
  waiting for transfers between devices  45.6 us (21%)
  local copies, waits for them, and re-layouts  26.5 us (12%)
  between operations  14.9 us (7%)
  starting transfers between devices  7.14 us (3%)
  other arithmetic  4.79 us (2%)
    dot_general x1, matrix products, warp_pieces(): jnp.einsum('pij,pjk->pik', w_rows, k_rows, preferred_element_type=jnp.flo...  43.7 us
    dot_general x1, matrix products, warp_pieces(): jnp.einsum('pij,pjk->pik', w_cols, k_cols, preferred_element_type=jnp.flo...  40.1 us
    scatter x1, local copies, waits for them, and re-layouts, shards(): jnp.zeros((owners * capacity, 2, size), jnp.bfloat16).at[slot].set(vectors)  21 us
    reduce_scatter x1, waiting for transfers between devices, shards(): lax.psum_scatter(summed.reshape(1 * lax.axis_size('vis'), size, size), 'v...  20.3 us
    psum x1, waiting for transfers between devices, shards(): detection = lax.psum(band_gain[0] * coadd, 'band')  18 us
    dot_general x1, matrix products, warp_pieces(): jnp.einsum('pij,pjk->pik', left, inner, preferred_element_type=jnp.float32)  11.9 us
    dot_general x2, matrix products, kernel_matrix(): jnp.einsum('pt,tij->pij', kernel, table, precision=lax.Precision.HIGHEST)  10.7 us
    all_to_all x1, waiting for transfers between devices, shards(): lax.all_to_all(vec_buffer, 'vis', split_axis=0, concat_axis=0, tiled=True)  7.29 us
  transfers between devices with their start and end apart: 3, of which 3 were waited for; matrix products, arithmetic and copies ran while one was open for 13% of the time, Pallas kernels for 0%

commit v1 on v0

v1 whole, which is shorter than its diff:
```python
import functools
import math

import jax
import jax.numpy as jnp
from jax import lax
from jax.experimental import pallas as pl
from jax.experimental.pallas import tpu as pltpu
from jax.sharding import PartitionSpec as P

GROUP = 4
SIDE = 3
EDGE = 16
MESH = pl.DeviceIdType.MESH


def lanczos(x):
    inside = jnp.abs(x) < 3.0
    u = jnp.where(inside, x, 0.0) * (math.pi / 3.0)
    square = u * u
    q = jnp.full_like(square, -1.0 / math.factorial(23))
    for k in range(10, -1, -1):
        q = q * square + (-1.0 if k % 2 else 1.0) / math.factorial(2 * k + 1)
    q2 = q * q
    return jnp.where(inside, q2 * (1.0 - (4.0 / 3.0) * square * q2), 0.0)


def tap_rows(taps, shift, size):
    rows, count = taps.shape
    reach = (count - 1) // 2
    lane = lax.broadcasted_iota(jnp.int32, (rows, size), 1)
    k = taps / jnp.sum(taps, axis=1, keepdims=True)
    k = jnp.concatenate([k, jnp.zeros((rows, size - count), jnp.float32)], axis=1)
    k = k.astype(jnp.bfloat16).astype(jnp.float32)
    w = lanczos((lane - SIDE).astype(jnp.float32) - shift)
    w = jnp.where(lane <= 2 * SIDE, w, 0.0)
    w = w / jnp.sum(w, axis=1, keepdims=True)
    w = w.astype(jnp.bfloat16).astype(jnp.float32)
    terms = [
        w[:, m + SIDE : m + SIDE + 1] * pltpu.roll(k, (m - reach) % size, 1)
        for m in range(-SIDE, SIDE + 1)
    ]
    down = terms[6] + terms[5] + terms[4]
    first = []
    for m in range(SIDE, -1, -1):
        down = down + terms[m]
        first.append(down)
    up = terms[0] + terms[1] + terms[2]
    last = []
    for m in range(SIDE, 2 * SIDE):
        up = up + terms[m]
        last.append(up)
    return first + last


def band_matrix(ref, p, size, masks):
    sub, keep = masks
    row = [jnp.broadcast_to(ref[v, pl.ds(p, 1), :], (8, size)) for v in range(7)]
    top = jnp.where(sub == 0, row[0], jnp.where(sub == 1, row[1], jnp.where(sub == 2, row[2], row[3])))
    end = jnp.where(sub == 7, row[4], jnp.where(sub == 6, row[5], jnp.where(sub == 5, row[6], row[3])))
    base = pltpu.roll(row[3], 0, 1, stride=1, stride_axis=0)
    parts = []
    tiles = size // 8
    for v in range(tiles):
        if v == 0:
            x = pltpu.roll(top, 0, 1, stride=1, stride_axis=0)
        elif v == tiles - 1:
            x = pltpu.roll(end, size - 8, 1, stride=1, stride_axis=0)
        else:
            x = pltpu.roll(base, 8 * v, 1)
        if v in keep:
            x = jnp.where(keep[v], x, 0.0)
        parts.append(x)
    return [
        jnp.concatenate(parts[2 * v : 2 * v + 2], axis=0).astype(jnp.bfloat16)
        for v in range(tiles // 2)
    ]


def sums_kernel(
    tile_ref, visit_ref, calib_ref, weights_ref, words_ref, taps_ref, shifts_ref, pieces_ref,
    out_ref,
    pbuf, left_taps, right_taps, good, acc, dacc, lbuf, rbuf, ibuf, cbuf,
    slots, blk_tile, cnt, cur, sems,
):
    count, size, _ = pieces_ref.shape
    tiles = acc.shape[0]
    chunks = sems.shape[0]
    each = count // chunks
    copies = [
        pltpu.make_async_copy(
            pieces_ref.at[pl.ds(c * each, each)], pbuf.at[pl.ds(c * each, each)], sems.at[c]
        )
        for c in range(chunks)
    ]
    for copy in copies:
        copy.start()

    def clear_slot(i, carry):
        slots[i] = -1
        return carry

    lax.fori_loop(0, slots.shape[0], clear_slot, 0, unroll=8)

    def clear_blk(i, carry):
        blk_tile[i] = 0
        return carry

    lax.fori_loop(0, blk_tile.shape[0], clear_blk, 0, unroll=8)
    for t in range(tiles):
        cnt[t] = 0
        cur[t] = 0
        acc[t] = jnp.zeros((size, size), jnp.float32)
        dacc[t] = jnp.zeros((2 * EDGE, size), jnp.float32)
    lbuf[...] = jnp.zeros_like(lbuf)
    ibuf[...] = jnp.zeros_like(ibuf)
    cbuf[...] = jnp.zeros_like(cbuf)

    words = words_ref.shape[1]
    lane8 = lax.broadcasted_iota(jnp.int32, (8, size), 1)

    def prepare(c, used):
        start = pl.multiple_of(c * 8, 8)
        here = pl.ds(start, 8)
        for i in range(8):
            t = tile_ref[start + i]
            n = cnt[t]
            inside = n & (GROUP - 1)
            fresh = inside == 0
            b = jnp.where(fresh, used, cur[t])
            cur[t] = b
            blk_tile[b + 1] = t
            slots[b * GROUP + inside] = start + i
            cnt[t] = n + 1
            used = jnp.where(fresh, used + 1, used)
        for d, table in ((0, left_taps), (1, right_taps)):
            rows = tap_rows(taps_ref[here, d, :], shifts_ref[here, d : d + 1], size)
            for v in range(7):
                table[v, here, :] = rows[v]
        packed = words_ref[here, :]
        word = jnp.broadcast_to(packed[:, 0:1], (8, size))
        for k in range(1, words):
            word = jnp.where(lane8 >= 32 * k, packed[:, k : k + 1], word)
        bit = lax.shift_right_logical(word, lane8 & 31) & 1
        good[here, :] = bit.astype(jnp.float32)
        return used

    used = lax.fori_loop(0, count // 8, prepare, jnp.int32(0))

    sub = lax.broadcasted_iota(jnp.int32, (8, size), 0)
    gap = lane8 - sub
    reach = (taps_ref.shape[2] - 1) // 2 + SIDE
    last = size // 8 - 1
    keep = {v: jnp.abs(gap - 8 * v) <= reach for v in (0, 1, last - 1, last)}
    masks = (sub, keep)

    def piece_of(step, g):
        return jnp.maximum(slots[step * GROUP + g], 0)

    def weight_of(step, g):
        p = slots[step * GROUP + g]
        v = visit_ref[jnp.maximum(p, 0)]
        w = jnp.where(p >= 0, weights_ref[v], 0).astype(jnp.float32)
        return w, w * calib_ref[v]

    def build_right(step):
        for g in range(GROUP):
            p = piece_of(step, g)
            mask = jnp.broadcast_to(good[pl.ds(p, 1), :], (16, size)).astype(jnp.bfloat16)
            parts = band_matrix(right_taps, p, size, masks)
            for v, part in enumerate(parts):
                rbuf[g, 16 * v : 16 * v + 16, :] = part * mask

    def build_left(step):
        for g in range(GROUP):
            p = piece_of(step, g)
            parts = band_matrix(left_taps, p, size, masks)
            for v, part in enumerate(parts):
                lbuf[16 * v : 16 * v + 16, g * size : (g + 1) * size] = part

    for copy in copies:
        copy.wait()
    build_right(0)
    ones = jnp.ones((16, size), jnp.bfloat16)

    def step_body(k, carry):
        t = blk_tile[k]
        part = jnp.dot(lbuf[...], ibuf[...], preferred_element_type=jnp.float32)
        acc[t] = acc[t] + part
        den = dacc[t]
        for g in range(GROUP):
            cols = slice(g * size, (g + 1) * size)
            rim = jnp.concatenate(
                [lbuf[0:EDGE, cols], lbuf[size - EDGE : size, cols]], axis=0
            ).astype(jnp.float32)
            den = den + jnp.sum(rim, axis=1, keepdims=True) * cbuf[g, 0:1, :]
        dacc[t] = den
        for g in range(GROUP):
            p = piece_of(k, g)
            w, factor = weight_of(k, g)
            x = jnp.concatenate([pbuf[p], ones], axis=0)
            y = lax.dot_general(
                x, rbuf[g], (((1,), (1,)), ((), ())), preferred_element_type=jnp.float32
            )
            ibuf[g * size : (g + 1) * size, :] = (y[0:size] * factor).astype(jnp.bfloat16)
            cbuf[g] = y[size : size + 8] * w
        build_left(k)
        build_right(k + 1)
        return carry

    lax.fori_loop(0, used + 1, step_body, 0)
    for t in range(tiles):
        out_ref[t, 0:size, :] = acc[t].astype(jnp.bfloat16)
        out_ref[t, size : size + 2 * EDGE, :] = dacc[t].astype(jnp.bfloat16)


def local_sums(pieces, visit, tile, words, taps, shifts, calib, weights, tiles):
    count, size, _ = pieces.shape
    blocks = (count + tiles * (GROUP - 1)) // GROUP + 2
    smem = pl.BlockSpec(memory_space=pltpu.SMEM)
    vmem = pl.BlockSpec(memory_space=pltpu.VMEM)
    chunks = 8 if count % 8 == 0 else 1
    return pl.pallas_call(
        sums_kernel,
        out_shape=jax.ShapeDtypeStruct((tiles, size + 2 * EDGE, size), jnp.bfloat16),
        in_specs=[smem] * 4 + [vmem] * 3 + [pl.BlockSpec(memory_space=pl.ANY)],
        out_specs=vmem,
        scratch_shapes=[
            pltpu.VMEM((count, size, size), jnp.bfloat16),
            pltpu.VMEM((7, count, size), jnp.float32),
            pltpu.VMEM((7, count, size), jnp.float32),
            pltpu.VMEM((count, size), jnp.float32),
            pltpu.VMEM((tiles, size, size), jnp.float32),
            pltpu.VMEM((tiles, 2 * EDGE, size), jnp.float32),
            pltpu.VMEM((size, GROUP * size), jnp.bfloat16),
            pltpu.VMEM((GROUP, size, size), jnp.bfloat16),
            pltpu.VMEM((GROUP * size, size), jnp.bfloat16),
            pltpu.VMEM((GROUP, 8, size), jnp.float32),
            pltpu.SMEM((blocks * GROUP,), jnp.int32),
            pltpu.SMEM((blocks + 1,), jnp.int32),
            pltpu.SMEM((tiles,), jnp.int32),
            pltpu.SMEM((tiles,), jnp.int32),
            pltpu.SemaphoreType.DMA((chunks,)),
        ],
        compiler_params=pltpu.CompilerParams(vmem_limit_bytes=40 * 1024 * 1024),
        name="local_sums",
    )(tile, visit, calib, weights, words, taps, shifts, pieces)


def owner_kernel(
    owners, bands, gain_ref, sums_ref, coadd_ref, det_ref,
    got, mine, other, send_sem, recv_sem, band_send, band_recv,
):
    size = coadd_ref.shape[0]
    me = lax.axis_index("vis")
    band = lax.axis_index("band")
    barrier = pltpu.get_barrier_semaphore()
    for o in range(1, owners):
        pl.semaphore_signal(
            barrier, inc=1, device_id={"vis": lax.rem(me + o, owners)}, device_id_type=MESH
        )
    for o in range(1, bands):
        pl.semaphore_signal(
            barrier, inc=1, device_id={"band": lax.rem(band + o, bands)}, device_id_type=MESH
        )
    pl.semaphore_wait(barrier, owners + bands - 2)
    copies = []
    for o in range(1, owners):
        to = lax.rem(me + o, owners)
        copy = pltpu.make_async_remote_copy(
            src_ref=sums_ref.at[to],
            dst_ref=got.at[o],
            send_sem=send_sem.at[o],
            recv_sem=recv_sem.at[o],
            device_id={"vis": to},
            device_id_type=MESH,
        )
        copy.start()
        copies.append(copy)
    total = sums_ref[me].astype(jnp.float32)
    for o in range(1, owners):
        copies[o - 1].wait_recv()
        total = total + got[o].astype(jnp.float32)
    num = total[0:size]
    rim = jnp.maximum(total[size:], 1.0)
    inner = jnp.broadcast_to(rim[EDGE - 1 : EDGE], (size - 2 * EDGE, size))
    den = jnp.concatenate([rim[:EDGE], inner, rim[EDGE:]], axis=0)
    coadd = num / den
    coadd_ref[...] = coadd
    scaled = coadd * gain_ref[0]
    mine[...] = scaled
    swaps = []
    for o in range(1, bands):
        swap = pltpu.make_async_remote_copy(
            src_ref=mine,
            dst_ref=other.at[o],
            send_sem=band_send.at[o],
            recv_sem=band_recv.at[o],
            device_id={"band": lax.rem(band + o, bands)},
            device_id_type=MESH,
        )
        swap.start()
        swaps.append(swap)
    for o in range(1, bands):
        swaps[o - 1].wait_recv()
        scaled = scaled + other[o]
    det_ref[...] = scaled
    for copy in copies + swaps:
        copy.wait_send()


def owner_coadd(gain, sums, owners, bands):
    tiles, rows, size = sums.shape
    vmem = pl.BlockSpec(memory_space=pltpu.VMEM)
    out = jax.ShapeDtypeStruct((size, size), jnp.float32)
    return pl.pallas_call(
        functools.partial(owner_kernel, owners, bands),
        out_shape=(out, out),
        in_specs=[pl.BlockSpec(memory_space=pltpu.SMEM), vmem],
        out_specs=(vmem, vmem),
        scratch_shapes=[
            pltpu.VMEM((owners, rows, size), jnp.bfloat16),
            pltpu.VMEM((size, size), jnp.float32),
            pltpu.VMEM((bands, size, size), jnp.float32),
            pltpu.SemaphoreType.DMA((owners,)),
            pltpu.SemaphoreType.DMA((owners,)),
            pltpu.SemaphoreType.DMA((bands,)),
            pltpu.SemaphoreType.DMA((bands,)),
        ],
        compiler_params=pltpu.CompilerParams(
            collective_id=0, has_side_effects=True, vmem_limit_bytes=32 * 1024 * 1024
        ),
        name="owner_coadd",
    )(gain, sums)


def shards(pieces, visit, tile_map, good_columns, psf_taps, shifts, calib, weights, band_gain):
    owners = lax.axis_size("vis")
    sums = local_sums(
        pieces[0], visit[0], tile_map[0, :, 0], good_columns[0], psf_taps[0], shifts[0],
        calib[0], weights[0], owners,
    )
    coadd, detection = owner_coadd(band_gain, sums, owners, lax.axis_size("band"))
    return (coadd[None], detection)


def solution(mesh):
    placed = (
        P("band", ("groups", "vis"), None, None),
        P("band", ("groups", "vis")),
        P("band", ("groups", "vis"), None),
        P("band", ("groups", "vis"), None),
        P("band", ("groups", "vis"), None, None),
        P("band", ("groups", "vis"), None),
        P("band", None),
        P("band", None),
        P("band"),
    )
    return jax.shard_map(
        shards,
        mesh=mesh,
        in_specs=placed,
        out_specs=(P("band", ("groups", "vis"), None), P(("groups", "vis"), None)),
        check_vma=False,
    )
```

time: 221 us -> 51.8 us (0.23)
  matrix products: 122 us -> 0 us
  waiting for transfers between devices: 45.6 us -> 0 us
  Pallas kernels: 0 us -> 40.8 us
  local copies, waits for them, and re-layouts: 26.5 us -> 9.23 us
  between operations: 14.9 us -> 1.33 us
  starting transfers between devices: 7.14 us -> 0 us
  other arithmetic: 4.79 us -> 0 us
    dot_general x9 -> x0, matrix products: 122 us -> none  [the longest x1 43.7 us: warp_pieces(): jnp.einsum('pij,pjk->pik', w_rows, k_rows, preferred_element_type=jnp.flo...]
    pallas_call x0 -> x2, Pallas kernels: none -> 40.8 us  [the longest x1 27.6 us: local_sums(): pl.pallas_call(sums_kernel, out_shape=jax.ShapeDtypeStruct((tiles, size +...]
    scatter x1 -> x0, local copies, waits for them, and re-layouts: 21 us -> none  [shards(): jnp.zeros((owners * capacity, 2, size), jnp.bfloat16).at[slot].set(vectors)]
    reduce_scatter x1 -> x0, waiting for transfers between devices: 20.3 us -> none  [shards(): lax.psum_scatter(summed.reshape(1 * lax.axis_size('vis'), size, size), 'v...]
    psum x1 -> x0, waiting for transfers between devices: 18 us -> none  [shards(): detection = lax.psum(band_gain[0] * coadd, 'band')]
    unnamed x15, local copies, waits for them, and re-layouts: 1.51 us -> 9.23 us
    all_to_all x1 -> x0, waiting for transfers between devices: 7.29 us -> none  [shards(): lax.all_to_all(vec_buffer, 'vis', split_axis=0, concat_axis=0, tiled=True)]
    all_to_all x1 -> x0, starting transfers between devices: 7.06 us -> none  [shards(): lax.all_to_all(vec_buffer, 'vis', split_axis=0, concat_axis=0, tiled=True)]
  transfers between devices with their start and end apart: 3 -> 0, of which waited for: 3 -> 0; matrix products, arithmetic and copies ran while one was open for 13% -> 0% of each run, Pallas kernels for 0% -> 0%
where the time goes in v1:
time: 51.8 us; the launch traced here: 51.4 us
  Pallas kernels  40.8 us (79%)
  local copies, waits for them, and re-layouts  9.23 us (18%)
  between operations  1.33 us (3%)
    pallas_call x1, Pallas kernels, local_sums(): pl.pallas_call(sums_kernel, out_shape=jax.ShapeDtypeStruct((tiles, size +...  27.6 us
    pallas_call x1, Pallas kernels, owner_coadd(): pl.pallas_call(functools.partial(owner_kernel, owners, bands), out_shape=...  13.2 us
    unnamed x15, local copies, waits for them, and re-layouts  9.23 us

profile of v1, /device:TPU:0, one launch (start us, length us, event | category | flops | bytes accessed | tf_op | source)
XLA Modules:
  0.0 51.4 jit_solution(11056066964415982448)
XLA Ops:
  0.6 0.9 %copy.12 = f32[1,192,2,21]{3,2,1,0:T(2,128)S(1)} copy(f32[1,192,2,21]{1,2,3,0:T(2,128)} %param.13) | data formatting | bytes 64512 | tf_op args[4]
  1.6 0.8 %copy.11 = s32[1,192,4]{2,1,0:T(8,128)S(1)} copy(s32[1,192,4]{1,2,0:T(4,128)} %param.12) | data formatting | bytes 6144 | tf_op args[3]
  2.4 0.8 %copy.13 = f32[1,192,2]{2,1,0:T(8,128)S(1)} copy(f32[1,192,2]{1,2,0:T(2,128)} %param.14) | data formatting | bytes 3072 | tf_op args[5]
  3.2 0.0 copy-start
  3.2 2.8 %copy-done = bf16[1,192,128,128]{3,2,1,0:T(8,128)(2,1)S(1)} copy-done((bf16[1,192,128,128]{3,2,1,0:T(8,128)(2,1)S(1)}, bf16[1,192,128,128]{3,2,1,0:T(8,128)(2,1)}, u32[]{:S(2)}) %copy-start) | copy-done | bytes 6291480
  6.0 0.0 copy-start.1
  6.0 0.7 %copy-done.1 = s32[1,192,1]{1,2,0:T(1,128)S(1)} copy-done((s32[1,192,1]{1,2,0:T(1,128)S(1)}, s32[1,192,1]{1,2,0:T(1,128)}, u32[]{:S(2)}) %copy-start.1) | copy-done | bytes 792
  6.6 0.0 copy-start.2
  6.6 0.7 %copy-done.2 = s32[1,192]{1,0:T(1,128)S(1)} copy-done((s32[1,192]{1,0:T(1,128)S(1)}, s32[1,192]{1,0:T(1,128)}, u32[]{:S(2)}) %copy-start.2) | copy-done | bytes 792
  7.3 0.0 copy-start.3
  7.3 0.7 %copy-done.3 = f32[1,24]{1,0:T(1,128)S(1)} copy-done((f32[1,24]{1,0:T(1,128)S(1)}, f32[1,24]{1,0:T(1,128)}, u32[]{:S(2)}) %copy-start.3) | copy-done | bytes 120
  8.0 0.0 copy-start.4
  8.0 0.7 %copy-done.4 = s32[1,24]{1,0:T(1,128)S(1)} copy-done((s32[1,24]{1,0:T(1,128)S(1)}, s32[1,24]{1,0:T(1,128)}, u32[]{:S(2)}) %copy-start.4) | copy-done | bytes 120
  8.6 27.6 %local_sums.1.sums_ref = bf16[8,160,128]{2,1,0:T(8,128)(2,1)S(1)} custom-call(s32[192]{0:T(256)S(1)} %bitcast.14, s32[192]{0:T(256)S(1)} %bitcast.15, f32[24]{0:T(128)S(1)} %bitcast.16, s32[24]{0:T(128)S(1)} %bitcast.17, s32[192,4]{1,0:T(8,128)S(1)} %bitcast.11, f32[192,2,21]{2,1,0:T(2,128)S(1)} %bitcast.10, f32[192,2]{1,0:T(8,128)S(1)} %bitcast.12, ...), custom_call_target="tpu_custom_call" | custom-call | tf_op jit(solution)/shard_map/local_sums/pallas_call | solution.py:223
  36.9 13.2 %owner_coadd.1 = (f32[128,128]{1,0:T(8,128)S(1)}, f32[128,128]{1,0:T(8,128)S(1)}) custom-call(f32[1]{0:T(128)S(6)} %copy.16.gain_ref, bf16[8,160,128]{2,1,0:T(8,128)(2,1)S(1)} %local_sums.1.sums_ref), custom_call_target="tpu_custom_call" | custom-call | tf_op jit(solution)/shard_map/owner_coadd/pallas_call | solution.py:316
  50.1 0.6 %copy.17 = f32[1,128,128]{2,1,0:T(8,128)} copy(f32[1,128,128]{2,1,0:T(8,128)S(1)} %bitcast.13) | data formatting | bytes 131072
  50.7 0.6 %copy.18 = f32[128,128]{1,0:T(8,128)} copy(f32[128,128]{1,0:T(8,128)S(1)} %get-tuple-element.9) | data formatting | bytes 131072
Async XLA Ops:
  3.2 2.8 %copy-start = (bf16[1,192,128,128]{3,2,1,0:T(8,128)(2,1)S(1)}, bf16[1,192,128,128]{3,2,1,0:T(8,128)(2,1)}, u32[]{:S(2)}) copy-start(bf16[1,192,128,128]{3,2,1,0:T(8,128)(2,1)} %param.9) | copy-start | bytes 18874372
  6.0 0.7 %copy-start.1 = (s32[1,192,1]{1,2,0:T(1,128)S(1)}, s32[1,192,1]{1,2,0:T(1,128)}, u32[]{:S(2)}) copy-start(s32[1,192,1]{1,2,0:T(1,128)} %param.11) | copy-start | bytes 2308
  6.6 0.7 %copy-start.2 = (s32[1,192]{1,0:T(1,128)S(1)}, s32[1,192]{1,0:T(1,128)}, u32[]{:S(2)}) copy-start(s32[1,192]{1,0:T(1,128)} %param.10) | copy-start | bytes 2308
  7.3 0.7 %copy-start.3 = (f32[1,24]{1,0:T(1,128)S(1)}, f32[1,24]{1,0:T(1,128)}, u32[]{:S(2)}) copy-start(f32[1,24]{1,0:T(1,128)} %param.15) | copy-start | bytes 292
  8.0 0.7 %copy-start.4 = (s32[1,24]{1,0:T(1,128)S(1)}, s32[1,24]{1,0:T(1,128)}, u32[]{:S(2)}) copy-start(s32[1,24]{1,0:T(1,128)} %param.16) | copy-start | bytes 292

commit v2 on v1

--- a/solution.py
+++ b/solution.py
@@ -25,19 +25,14 @@
     return jnp.where(inside, q2 * (1.0 - (4.0 / 3.0) * square * q2), 0.0)
 
 
-def tap_rows(taps, shift, size):
-    rows, count = taps.shape
-    reach = (count - 1) // 2
-    lane = lax.broadcasted_iota(jnp.int32, (rows, size), 1)
-    k = taps / jnp.sum(taps, axis=1, keepdims=True)
-    k = jnp.concatenate([k, jnp.zeros((rows, size - count), jnp.float32)], axis=1)
-    k = k.astype(jnp.bfloat16).astype(jnp.float32)
-    w = lanczos((lane - SIDE).astype(jnp.float32) - shift)
-    w = jnp.where(lane <= 2 * SIDE, w, 0.0)
-    w = w / jnp.sum(w, axis=1, keepdims=True)
+def tap_columns(padded, shift, width):
+    sub = lax.broadcasted_iota(jnp.int32, (8, shift.shape[1]), 0)
+    w = lanczos((sub - SIDE).astype(jnp.float32) - shift)
+    w = jnp.where(sub <= 2 * SIDE, w, 0.0)
+    w = w / jnp.sum(w, axis=0, keepdims=True)
     w = w.astype(jnp.bfloat16).astype(jnp.float32)
     terms = [
-        w[:, m + SIDE : m + SIDE + 1] * pltpu.roll(k, (m - reach) % size, 1)
+        w[m + SIDE : m + SIDE + 1] * padded[SIDE - m : SIDE - m + width, :]
         for m in range(-SIDE, SIDE + 1)
     ]
     down = terms[6] + terms[5] + terms[4]
@@ -50,7 +45,7 @@
     for m in range(SIDE, 2 * SIDE):
         up = up + terms[m]
         last.append(up)
-    return first + last
+    return first, last
 
 
 def band_matrix(ref, p, size, masks):
@@ -59,34 +54,46 @@
     top = jnp.where(sub == 0, row[0], jnp.where(sub == 1, row[1], jnp.where(sub == 2, row[2], row[3])))
     end = jnp.where(sub == 7, row[4], jnp.where(sub == 6, row[5], jnp.where(sub == 5, row[6], row[3])))
     base = pltpu.roll(row[3], 0, 1, stride=1, stride_axis=0)
-    parts = []
+    top = pltpu.roll(top, 0, 1, stride=1, stride_axis=0)
+    end = pltpu.roll(end, size - 8, 1, stride=1, stride_axis=0)
     tiles = size // 8
-    for v in range(tiles):
-        if v == 0:
-            x = pltpu.roll(top, 0, 1, stride=1, stride_axis=0)
-        elif v == tiles - 1:
-            x = pltpu.roll(end, size - 8, 1, stride=1, stride_axis=0)
-        else:
-            x = pltpu.roll(base, 8 * v, 1)
-        if v in keep:
-            x = jnp.where(keep[v], x, 0.0)
-        parts.append(x)
-    return [
-        jnp.concatenate(parts[2 * v : 2 * v + 2], axis=0).astype(jnp.bfloat16)
-        for v in range(tiles // 2)
+    next8 = pltpu.roll(base, 8, 1)
+    head = [jnp.where(keep[0], top, 0.0), jnp.where(keep[1], next8, 0.0)]
+    tail = [
+        jnp.where(keep[tiles - 2], pltpu.roll(base, size - 16, 1), 0.0),
+        jnp.where(keep[tiles - 1], end, 0.0),
     ]
+    pair = jnp.concatenate([base, next8], axis=0).astype(jnp.bfloat16)
+    parts = [jnp.concatenate(head, axis=0).astype(jnp.bfloat16)]
+    for v in range(1, tiles // 2 - 1):
+        parts.append(pltpu.roll(pair, 16 * v, 1))
+    parts.append(jnp.concatenate(tail, axis=0).astype(jnp.bfloat16))
+    return parts
 
 
 def sums_kernel(
-    tile_ref, visit_ref, calib_ref, weights_ref, words_ref, taps_ref, shifts_ref, pieces_ref,
+    tile_hbm, visit_hbm, calib_hbm, weights_hbm, words_hbm, taps_hbm, shifts_hbm, pieces_ref,
     out_ref,
-    pbuf, left_taps, right_taps, good, acc, dacc, lbuf, rbuf, ibuf, cbuf,
-    slots, blk_tile, cnt, cur, sems,
+    pbuf, words_ref, taps_ref, shifts_ref, padded, columns, left_taps, right_taps, good,
+    acc, dacc, lbuf, rbuf, ibuf, cbuf,
+    tile_ref, visit_ref, calib_ref, weights_ref, slots, blk_tile, cnt, cur, sems, small_sems,
 ):
     count, size, _ = pieces_ref.shape
     tiles = acc.shape[0]
     chunks = sems.shape[0]
     each = count // chunks
+    smalls = [
+        pltpu.make_async_copy(src, dst, small_sems.at[i])
+        for i, (src, dst) in enumerate(
+            (
+                (tile_hbm, tile_ref), (shifts_hbm, shifts_ref), (taps_hbm, taps_ref),
+                (words_hbm, words_ref), (visit_hbm, visit_ref), (calib_hbm, calib_ref),
+                (weights_hbm, weights_ref),
+            )
+        )
+    ]
+    for copy in smalls:
+        copy.start()
     copies = [
         pltpu.make_async_copy(
             pieces_ref.at[pl.ds(c * each, each)], pbuf.at[pl.ds(c * each, each)], sems.at[c]
@@ -115,43 +122,64 @@
     lbuf[...] = jnp.zeros_like(lbuf)
     ibuf[...] = jnp.zeros_like(ibuf)
     cbuf[...] = jnp.zeros_like(cbuf)
-
-    words = words_ref.shape[1]
-    lane8 = lax.broadcasted_iota(jnp.int32, (8, size), 1)
-
-    def prepare(c, used):
-        start = pl.multiple_of(c * 8, 8)
-        here = pl.ds(start, 8)
-        for i in range(8):
-            t = tile_ref[start + i]
-            n = cnt[t]
-            inside = n & (GROUP - 1)
-            fresh = inside == 0
-            b = jnp.where(fresh, used, cur[t])
-            cur[t] = b
-            blk_tile[b + 1] = t
-            slots[b * GROUP + inside] = start + i
-            cnt[t] = n + 1
-            used = jnp.where(fresh, used + 1, used)
-        for d, table in ((0, left_taps), (1, right_taps)):
-            rows = tap_rows(taps_ref[here, d, :], shifts_ref[here, d : d + 1], size)
-            for v in range(7):
-                table[v, here, :] = rows[v]
-        packed = words_ref[here, :]
-        word = jnp.broadcast_to(packed[:, 0:1], (8, size))
-        for k in range(1, words):
-            word = jnp.where(lane8 >= 32 * k, packed[:, k : k + 1], word)
-        bit = lax.shift_right_logical(word, lane8 & 31) & 1
-        good[here, :] = bit.astype(jnp.float32)
-        return used
-
-    used = lax.fori_loop(0, count // 8, prepare, jnp.int32(0))
+    padded[...] = jnp.zeros_like(padded)
+    for copy in smalls:
+        copy.wait()
+
+    def place(i, used):
+        t = tile_ref[0, i]
+        n = cnt[t]
+        inside = n & (GROUP - 1)
+        fresh = inside == 0
+        b = jnp.where(fresh, used, cur[t])
+        cur[t] = b
+        blk_tile[b + 1] = t
+        slots[b * GROUP + inside] = i
+        cnt[t] = n + 1
+        return jnp.where(fresh, used + 1, used)
+
+    used = lax.fori_loop(0, count, place, jnp.int32(0), unroll=8)
+
+    taps_count = taps_ref.shape[0]
+    reach = (taps_count - 1) // 2 + SIDE
+    block = size // 4
+    wide = padded.shape[2]
+    place_lane = lax.broadcasted_iota(jnp.int32, (size, size), 1)
+    inside = (place_lane < block - reach) | (place_lane >= size - reach)
+    for d, table in ((0, left_taps), (1, right_taps)):
+        taps = taps_ref[:, d, :]
+        kernel = taps / jnp.sum(taps, axis=0, keepdims=True)
+        kernel = kernel.astype(jnp.bfloat16).astype(jnp.float32)
+        padded[d, 2 * SIDE : 2 * SIDE + taps_count, 0:count] = kernel
+        shift = jnp.concatenate(
+            [shifts_ref[d : d + 1, :], jnp.zeros((1, wide - count), jnp.float32)], axis=1
+        )
+        first, last = tap_columns(padded.at[d], shift, block)
+        for v, rows in enumerate(first):
+            columns[0, block * v : block * (v + 1), :] = rows
+        for v, rows in enumerate(last):
+            columns[1, block * v : block * (v + 1), :] = rows
+        columns[1, 3 * block : size, :] = first[3]
+        for h in range(2):
+            for c in range(wide // size):
+                part = columns[h, :, c * size : (c + 1) * size]
+                turned = part.T
+                for v in range(4 if h == 0 else 3):
+                    x = pltpu.roll(turned, (-block * v - reach) % size, 1)
+                    table[4 * h + v, c * size : (c + 1) * size, :] = jnp.where(inside, x, 0.0)
+    bit = lax.broadcasted_iota(jnp.int32, (32, count), 0)
+    flags = [
+        (lax.shift_right_logical(jnp.broadcast_to(words_ref[k : k + 1, :], (32, count)), bit) & 1)
+        for k in range(size // 32)
+    ]
+    columns[0, :, 0:count] = jnp.concatenate(flags, axis=0).astype(jnp.float32)
+    for c in range(wide // size):
+        good[c * size : (c + 1) * size, :] = columns[0, :, c * size : (c + 1) * size].T
 
     sub = lax.broadcasted_iota(jnp.int32, (8, size), 0)
-    gap = lane8 - sub
-    reach = (taps_ref.shape[2] - 1) // 2 + SIDE
-    last = size // 8 - 1
-    keep = {v: jnp.abs(gap - 8 * v) <= reach for v in (0, 1, last - 1, last)}
+    lane = lax.broadcasted_iota(jnp.int32, (8, size), 1)
+    final = size // 8 - 1
+    keep = {v: jnp.abs(lane - sub - 8 * v) <= reach for v in (0, 1, final - 1, final)}
     masks = (sub, keep)
 
     def piece_of(step, g):
@@ -159,9 +187,9 @@
 
     def weight_of(step, g):
         p = slots[step * GROUP + g]
-        v = visit_ref[jnp.maximum(p, 0)]
-        w = jnp.where(p >= 0, weights_ref[v], 0).astype(jnp.float32)
-        return w, w * calib_ref[v]
+        v = visit_ref[0, jnp.maximum(p, 0)]
+        w = jnp.where(p >= 0, weights_ref[0, v], 0).astype(jnp.float32)
+        return w, w * calib_ref[0, v]
 
     def build_right(step):
         for g in range(GROUP):
@@ -217,43 +245,57 @@
 def local_sums(pieces, visit, tile, words, taps, shifts, calib, weights, tiles):
     count, size, _ = pieces.shape
     blocks = (count + tiles * (GROUP - 1)) // GROUP + 2
-    smem = pl.BlockSpec(memory_space=pltpu.SMEM)
-    vmem = pl.BlockSpec(memory_space=pltpu.VMEM)
+    hbm = pl.BlockSpec(memory_space=pltpu.HBM)
     chunks = 8 if count % 8 == 0 else 1
+    wide = -(-count // size) * size
     return pl.pallas_call(
         sums_kernel,
         out_shape=jax.ShapeDtypeStruct((tiles, size + 2 * EDGE, size), jnp.bfloat16),
-        in_specs=[smem] * 4 + [vmem] * 3 + [pl.BlockSpec(memory_space=pl.ANY)],
-        out_specs=vmem,
+        in_specs=[hbm] * 8,
+        out_specs=pl.BlockSpec(memory_space=pltpu.VMEM),
         scratch_shapes=[
             pltpu.VMEM((count, size, size), jnp.bfloat16),
-            pltpu.VMEM((7, count, size), jnp.float32),
-            pltpu.VMEM((7, count, size), jnp.float32),
-            pltpu.VMEM((count, size), jnp.float32),
+            pltpu.VMEM(words.shape, jnp.int32),
+            pltpu.VMEM(taps.shape, jnp.float32),
+            pltpu.VMEM(shifts.shape, jnp.float32),
+            pltpu.VMEM((2, size // 4 + 8, wide), jnp.float32),
+            pltpu.VMEM((2, size, wide), jnp.float32),
+            pltpu.VMEM((7, wide, size), jnp.float32),
+            pltpu.VMEM((7, wide, size), jnp.float32),
+            pltpu.VMEM((wide, size), jnp.float32),
             pltpu.VMEM((tiles, size, size), jnp.float32),
             pltpu.VMEM((tiles, 2 * EDGE, size), jnp.float32),
             pltpu.VMEM((size, GROUP * size), jnp.bfloat16),
             pltpu.VMEM((GROUP, size, size), jnp.bfloat16),
             pltpu.VMEM((GROUP * size, size), jnp.bfloat16),
             pltpu.VMEM((GROUP, 8, size), jnp.float32),
+            pltpu.SMEM(tile.shape, jnp.int32),
+            pltpu.SMEM(visit.shape, jnp.int32),
+            pltpu.SMEM(calib.shape, jnp.float32),
+            pltpu.SMEM(weights.shape, jnp.int32),
             pltpu.SMEM((blocks * GROUP,), jnp.int32),
             pltpu.SMEM((blocks + 1,), jnp.int32),
             pltpu.SMEM((tiles,), jnp.int32),
             pltpu.SMEM((tiles,), jnp.int32),
             pltpu.SemaphoreType.DMA((chunks,)),
+            pltpu.SemaphoreType.DMA((7,)),
         ],
-        compiler_params=pltpu.CompilerParams(vmem_limit_bytes=40 * 1024 * 1024),
+        compiler_params=pltpu.CompilerParams(vmem_limit_bytes=56 * 1024 * 1024),
         name="local_sums",
     )(tile, visit, calib, weights, words, taps, shifts, pieces)
 
 
 def owner_kernel(
     owners, bands, gain_ref, sums_ref, coadd_ref, det_ref,
-    got, mine, other, send_sem, recv_sem, band_send, band_recv,
+    own, got, mine, other, gain, own_sem, send_sem, recv_sem, band_send, band_recv, gain_sem,
 ):
     size = coadd_ref.shape[0]
+    load = pltpu.make_async_copy(gain_ref, gain, gain_sem)
+    load.start()
     me = lax.axis_index("vis")
     band = lax.axis_index("band")
+    keep = pltpu.make_async_copy(sums_ref.at[me], own, own_sem)
+    keep.start()
     barrier = pltpu.get_barrier_semaphore()
     for o in range(1, owners):
         pl.semaphore_signal(
@@ -277,7 +319,8 @@
         )
         copy.start()
         copies.append(copy)
-    total = sums_ref[me].astype(jnp.float32)
+    keep.wait()
+    total = own[...].astype(jnp.float32)
     for o in range(1, owners):
         copies[o - 1].wait_recv()
         total = total + got[o].astype(jnp.float32)
@@ -287,7 +330,8 @@
     den = jnp.concatenate([rim[:EDGE], inner, rim[EDGE:]], axis=0)
     coadd = num / den
     coadd_ref[...] = coadd
-    scaled = coadd * gain_ref[0]
+    load.wait()
+    scaled = coadd * gain[0, 0]
     mine[...] = scaled
     swaps = []
     for o in range(1, bands):
@@ -316,19 +360,23 @@
     return pl.pallas_call(
         functools.partial(owner_kernel, owners, bands),
         out_shape=(out, out),
-        in_specs=[pl.BlockSpec(memory_space=pltpu.SMEM), vmem],
+        in_specs=[pl.BlockSpec(memory_space=pltpu.HBM)] * 2,
         out_specs=(vmem, vmem),
         scratch_shapes=[
+            pltpu.VMEM((rows, size), jnp.bfloat16),
             pltpu.VMEM((owners, rows, size), jnp.bfloat16),
             pltpu.VMEM((size, size), jnp.float32),
             pltpu.VMEM((bands, size, size), jnp.float32),
+            pltpu.SMEM((1, 1), jnp.float32),
+            pltpu.SemaphoreType.DMA,
             pltpu.SemaphoreType.DMA((owners,)),
             pltpu.SemaphoreType.DMA((owners,)),
             pltpu.SemaphoreType.DMA((bands,)),
             pltpu.SemaphoreType.DMA((bands,)),
+            pltpu.SemaphoreType.DMA,
         ],
         compiler_params=pltpu.CompilerParams(
-            collective_id=0, has_side_effects=True, vmem_limit_bytes=32 * 1024 * 1024
+            collective_id=0, has_side_effects=True, vmem_limit_bytes=56 * 1024 * 1024
         ),
         name="owner_coadd",
     )(gain, sums)
@@ -337,10 +385,10 @@
 def shards(pieces, visit, tile_map, good_columns, psf_taps, shifts, calib, weights, band_gain):
     owners = lax.axis_size("vis")
     sums = local_sums(
-        pieces[0], visit[0], tile_map[0, :, 0], good_columns[0], psf_taps[0], shifts[0],
-        calib[0], weights[0], owners,
+        pieces[0], visit, tile_map[:, :, 0], good_columns[0].T, psf_taps[0].transpose(2, 1, 0),
+        shifts[0].T, calib, weights, owners,
     )
-    coadd, detection = owner_coadd(band_gain, sums, owners, lax.axis_size("band"))
+    coadd, detection = owner_coadd(band_gain.reshape(1, 1), sums, owners, lax.axis_size("band"))
     return (coadd[None], detection)
 
 

time: 51.8 us -> 39.6 us (0.76)
  local copies, waits for them, and re-layouts: 9.23 us -> 2.95 us
  Pallas kernels: 40.8 us -> 34.7 us
    pallas_call x1, Pallas kernels: 27.6 us -> 20.7 us  [local_sums(): pl.pallas_call(sums_kernel, out_shape=jax.ShapeDtypeStruct((tiles, size +...]
    unnamed x15 -> x2, local copies, waits for them, and re-layouts: 9.23 us -> 2.95 us
    pallas_call x1, Pallas kernels: 13.2 us -> 14 us  [owner_coadd(): pl.pallas_call(functools.partial(owner_kernel, owners, bands), out_shape=...]
where the time goes in v2:
time: 39.6 us; the launch traced here: 39 us
  Pallas kernels  34.7 us (88%)
  local copies, waits for them, and re-layouts  2.95 us (7%)
  between operations  1.3 us (3%)
    pallas_call x1, Pallas kernels, local_sums(): pl.pallas_call(sums_kernel, out_shape=jax.ShapeDtypeStruct((tiles, size +...  20.7 us
    pallas_call x1, Pallas kernels, owner_coadd(): pl.pallas_call(functools.partial(owner_kernel, owners, bands), out_shape=...  14 us
    unnamed x2, local copies, waits for them, and re-layouts  2.95 us

profile of v2, /device:TPU:0, one launch (start us, length us, event | category | flops | bytes accessed | tf_op | source)
XLA Modules:
  0.0 39.0 jit_solution(18284911629336168566)
XLA Ops:
  1.3 20.7 %local_sums.1.sums_ref = bf16[8,160,128]{2,1,0:T(8,128)(2,1)} custom-call(s32[1,192]{1,0:T(1,128)} %bitcast.19, s32[1,192]{1,0:T(1,128)} %visit_hbm.1, f32[1,24]{1,0:T(1,128)} %calib_hbm.1, s32[1,24]{1,0:T(1,128)} %weights_hbm.1, s32[4,192]{1,0:T(4,128)} %bitcast.17, f32[21,2,192]{2,1,0:T(2,128)} %bitcast.16, f32[2,192]{1,0:T(2,128)} %bitcast.18, ...), custom_call_target="tpu_custom_call" | custom-call | tf_op jit(solution)/shard_map/local_sums/pallas_call | solution.py:251
  22.0 14.0 %owner_coadd.1 = (f32[128,128]{1,0:T(8,128)}, f32[128,128]{1,0:T(8,128)}) custom-call(f32[1,1]{1,0:T(1,128)} %bitcast.13.gain_ref, bf16[8,160,128]{2,1,0:T(8,128)(2,1)} %local_sums.1.sums_ref), custom_call_target="tpu_custom_call" | custom-call | tf_op jit(solution)/shard_map/owner_coadd/pallas_call | solution.py:360
  36.0 1.5 %copy.14 = f32[1,128,128]{2,1,0:T(8,128)} copy(f32[1,128,128]{2,1,0:T(8,128)} %bitcast.15) | data formatting | bytes 131072
  37.5 1.5 %copy.15 = f32[128,128]{1,0:T(8,128)} copy(f32[128,128]{1,0:T(8,128)} %get-tuple-element.9) | data formatting | bytes 131072

commit v3 on v2

--- a/solution.py
+++ b/solution.py
@@ -8,7 +8,7 @@
 from jax.experimental.pallas import tpu as pltpu
 from jax.sharding import PartitionSpec as P
 
-GROUP = 4
+GROUP = 8
 SIDE = 3
 EDGE = 16
 MESH = pl.DeviceIdType.MESH
@@ -72,11 +72,11 @@
 
 
 def sums_kernel(
-    tile_hbm, visit_hbm, calib_hbm, weights_hbm, words_hbm, taps_hbm, shifts_hbm, pieces_ref,
-    out_ref,
+    tile_hbm, visit_hbm, calib_hbm, weights_hbm, gain_hbm, words_hbm, taps_hbm, shifts_hbm, pieces_ref,
+    out_ref, gain_out,
     pbuf, words_ref, taps_ref, shifts_ref, padded, columns, left_taps, right_taps, good,
     acc, dacc, lbuf, rbuf, ibuf, cbuf,
-    tile_ref, visit_ref, calib_ref, weights_ref, slots, blk_tile, cnt, cur, sems, small_sems,
+    tile_ref, visit_ref, calib_ref, weights_ref, gain_ref, slots, blk_tile, cnt, cur, sems, small_sems,
 ):
     count, size, _ = pieces_ref.shape
     tiles = acc.shape[0]
@@ -88,7 +88,7 @@
             (
                 (tile_hbm, tile_ref), (shifts_hbm, shifts_ref), (taps_hbm, taps_ref),
                 (words_hbm, words_ref), (visit_hbm, visit_ref), (calib_hbm, calib_ref),
-                (weights_hbm, weights_ref),
+                (weights_hbm, weights_ref), (gain_hbm, gain_ref),
             )
         )
     ]
@@ -126,6 +126,8 @@
     for copy in smalls:
         copy.wait()
 
+    gain_out[...] = jnp.full(gain_out.shape, gain_ref[0, 0])
+
     def place(i, used):
         t = tile_ref[0, i]
         n = cnt[t]
@@ -138,7 +140,9 @@
         cnt[t] = n + 1
         return jnp.where(fresh, used + 1, used)
 
-    used = lax.fori_loop(0, count, place, jnp.int32(0), unroll=8)
+    used = jnp.int32(0)
+    for i in range(count):
+        used = place(i, used)
 
     taps_count = taps_ref.shape[0]
     reach = (taps_count - 1) // 2 + SIDE
@@ -242,7 +246,7 @@
         out_ref[t, size : size + 2 * EDGE, :] = dacc[t].astype(jnp.bfloat16)
 
 
-def local_sums(pieces, visit, tile, words, taps, shifts, calib, weights, tiles):
+def local_sums(pieces, visit, tile, words, taps, shifts, calib, weights, gain, tiles):
     count, size, _ = pieces.shape
     blocks = (count + tiles * (GROUP - 1)) // GROUP + 2
     hbm = pl.BlockSpec(memory_space=pltpu.HBM)
@@ -250,9 +254,12 @@
     wide = -(-count // size) * size
     return pl.pallas_call(
         sums_kernel,
-        out_shape=jax.ShapeDtypeStruct((tiles, size + 2 * EDGE, size), jnp.bfloat16),
-        in_specs=[hbm] * 8,
-        out_specs=pl.BlockSpec(memory_space=pltpu.VMEM),
+        out_shape=(
+            jax.ShapeDtypeStruct((tiles, size + 2 * EDGE, size), jnp.bfloat16),
+            jax.ShapeDtypeStruct((8, size), jnp.float32),
+        ),
+        in_specs=[hbm] * 9,
+        out_specs=(pl.BlockSpec(memory_space=pltpu.VMEM),) * 2,
         scratch_shapes=[
             pltpu.VMEM((count, size, size), jnp.bfloat16),
             pltpu.VMEM(words.shape, jnp.int32),
@@ -273,57 +280,81 @@
             pltpu.SMEM(visit.shape, jnp.int32),
             pltpu.SMEM(calib.shape, jnp.float32),
             pltpu.SMEM(weights.shape, jnp.int32),
+            pltpu.SMEM(gain.shape, jnp.float32),
             pltpu.SMEM((blocks * GROUP,), jnp.int32),
             pltpu.SMEM((blocks + 1,), jnp.int32),
             pltpu.SMEM((tiles,), jnp.int32),
             pltpu.SMEM((tiles,), jnp.int32),
             pltpu.SemaphoreType.DMA((chunks,)),
-            pltpu.SemaphoreType.DMA((7,)),
+            pltpu.SemaphoreType.DMA((8,)),
         ],
         compiler_params=pltpu.CompilerParams(vmem_limit_bytes=56 * 1024 * 1024),
         name="local_sums",
-    )(tile, visit, calib, weights, words, taps, shifts, pieces)
+    )(tile, visit, calib, weights, gain, words, taps, shifts, pieces)
 
 
 def owner_kernel(
     owners, bands, gain_ref, sums_ref, coadd_ref, det_ref,
-    own, got, mine, other, gain, own_sem, send_sem, recv_sem, band_send, band_recv, gain_sem,
+    own, near, pair, far, mine, other, gain, gain_sem, own_sem,
+    near_send, near_recv, far_send, far_recv, band_send, band_recv,
 ):
     size = coadd_ref.shape[0]
+    half = owners // 2
+    me = lax.axis_index("vis")
+    band = lax.axis_index("band")
+    mate = me + 1 - 2 * lax.rem(me, 2)
     load = pltpu.make_async_copy(gain_ref, gain, gain_sem)
     load.start()
-    me = lax.axis_index("vis")
-    band = lax.axis_index("band")
-    keep = pltpu.make_async_copy(sums_ref.at[me], own, own_sem)
-    keep.start()
+    order = list(range(1, half)) + [0]
+    fetch = {}
+    for o in order:
+        fetch[o] = pltpu.make_async_copy(
+            sums_ref.at[lax.rem(me + 2 * o, owners)], own.at[o], own_sem.at[o]
+        )
+        fetch[o].start()
     barrier = pltpu.get_barrier_semaphore()
-    for o in range(1, owners):
+    pl.semaphore_signal(barrier, inc=1, device_id={"vis": mate}, device_id_type=MESH)
+    for o in range(1, half):
         pl.semaphore_signal(
-            barrier, inc=1, device_id={"vis": lax.rem(me + o, owners)}, device_id_type=MESH
+            barrier, inc=1, device_id={"vis": lax.rem(me + 2 * o, owners)}, device_id_type=MESH
         )
     for o in range(1, bands):
         pl.semaphore_signal(
             barrier, inc=1, device_id={"band": lax.rem(band + o, bands)}, device_id_type=MESH
         )
-    pl.semaphore_wait(barrier, owners + bands - 2)
-    copies = []
-    for o in range(1, owners):
-        to = lax.rem(me + o, owners)
-        copy = pltpu.make_async_remote_copy(
-            src_ref=sums_ref.at[to],
-            dst_ref=got.at[o],
-            send_sem=send_sem.at[o],
-            recv_sem=recv_sem.at[o],
-            device_id={"vis": to},
+    pl.semaphore_wait(barrier, half + bands - 1)
+    nears, fars = {}, {}
+    for o in order:
+        nears[o] = pltpu.make_async_remote_copy(
+            src_ref=sums_ref.at[lax.rem(mate + 2 * o, owners)],
+            dst_ref=near.at[o],
+            send_sem=near_send.at[o],
+            recv_sem=near_recv.at[o],
+            device_id={"vis": mate},
             device_id_type=MESH,
         )
-        copy.start()
-        copies.append(copy)
-    keep.wait()
-    total = own[...].astype(jnp.float32)
-    for o in range(1, owners):
-        copies[o - 1].wait_recv()
-        total = total + got[o].astype(jnp.float32)
+        nears[o].start()
+    total = None
+    for o in order:
+        fetch[o].wait()
+        nears[o].wait_recv()
+        both = own[o].astype(jnp.float32) + near[o].astype(jnp.float32)
+        if o == 0:
+            total = both
+            continue
+        pair[o] = both.astype(jnp.bfloat16)
+        fars[o] = pltpu.make_async_remote_copy(
+            src_ref=pair.at[o],
+            dst_ref=far.at[o],
+            send_sem=far_send.at[o],
+            recv_sem=far_recv.at[o],
+            device_id={"vis": lax.rem(me + 2 * o, owners)},
+            device_id_type=MESH,
+        )
+        fars[o].start()
+    for o in range(1, half):
+        fars[o].wait_recv()
+        total = total + far[o].astype(jnp.float32)
     num = total[0:size]
     rim = jnp.maximum(total[size:], 1.0)
     inner = jnp.broadcast_to(rim[EDGE - 1 : EDGE], (size - 2 * EDGE, size))
@@ -331,7 +362,7 @@
     coadd = num / den
     coadd_ref[...] = coadd
     load.wait()
-    scaled = coadd * gain[0, 0]
+    scaled = coadd * gain[0:1, :]
     mine[...] = scaled
     swaps = []
     for o in range(1, bands):
@@ -349,12 +380,13 @@
         swaps[o - 1].wait_recv()
         scaled = scaled + other[o]
     det_ref[...] = scaled
-    for copy in copies + swaps:
+    for copy in list(nears.values()) + list(fars.values()) + swaps:
         copy.wait_send()
 
 
 def owner_coadd(gain, sums, owners, bands):
     tiles, rows, size = sums.shape
+    half = owners // 2
     vmem = pl.BlockSpec(memory_space=pltpu.VMEM)
     out = jax.ShapeDtypeStruct((size, size), jnp.float32)
     return pl.pallas_call(
@@ -363,17 +395,21 @@
         in_specs=[pl.BlockSpec(memory_space=pltpu.HBM)] * 2,
         out_specs=(vmem, vmem),
         scratch_shapes=[
-            pltpu.VMEM((rows, size), jnp.bfloat16),
-            pltpu.VMEM((owners, rows, size), jnp.bfloat16),
+            pltpu.VMEM((half, rows, size), jnp.bfloat16),
+            pltpu.VMEM((half, rows, size), jnp.bfloat16),
+            pltpu.VMEM((half, rows, size), jnp.bfloat16),
+            pltpu.VMEM((half, rows, size), jnp.bfloat16),
             pltpu.VMEM((size, size), jnp.float32),
             pltpu.VMEM((bands, size, size), jnp.float32),
-            pltpu.SMEM((1, 1), jnp.float32),
+            pltpu.VMEM(gain.shape, jnp.float32),
             pltpu.SemaphoreType.DMA,
-            pltpu.SemaphoreType.DMA((owners,)),
-            pltpu.SemaphoreType.DMA((owners,)),
+            pltpu.SemaphoreType.DMA((half,)),
+            pltpu.SemaphoreType.DMA((half,)),
+            pltpu.SemaphoreType.DMA((half,)),
+            pltpu.SemaphoreType.DMA((half,)),
+            pltpu.SemaphoreType.DMA((half,)),
             pltpu.SemaphoreType.DMA((bands,)),
             pltpu.SemaphoreType.DMA((bands,)),
-            pltpu.SemaphoreType.DMA,
         ],
         compiler_params=pltpu.CompilerParams(
             collective_id=0, has_side_effects=True, vmem_limit_bytes=56 * 1024 * 1024
@@ -382,13 +418,32 @@
     )(gain, sums)
 
 
+def write_kernel(coadd_ref, det_ref, coadd_out, det_out):
+    coadd_out[...] = coadd_ref[...]
+    det_out[...] = det_ref[...]
+
+
+def write_out(coadd, detection):
+    vmem = pl.BlockSpec(memory_space=pltpu.VMEM)
+    out = jax.ShapeDtypeStruct(coadd.shape, coadd.dtype)
+    return pl.pallas_call(
+        write_kernel,
+        out_shape=(out, out),
+        in_specs=[vmem, vmem],
+        out_specs=(vmem, vmem),
+        compiler_params=pltpu.CompilerParams(vmem_limit_bytes=56 * 1024 * 1024),
+        name="write_out",
+    )(coadd, detection)
+
+
 def shards(pieces, visit, tile_map, good_columns, psf_taps, shifts, calib, weights, band_gain):
     owners = lax.axis_size("vis")
-    sums = local_sums(
+    sums, gain = local_sums(
         pieces[0], visit, tile_map[:, :, 0], good_columns[0].T, psf_taps[0].transpose(2, 1, 0),
-        shifts[0].T, calib, weights, owners,
+        shifts[0].T, calib, weights, band_gain.reshape(1, 1), owners,
     )
-    coadd, detection = owner_coadd(band_gain.reshape(1, 1), sums, owners, lax.axis_size("band"))
+    coadd, detection = owner_coadd(gain, sums, owners, lax.axis_size("band"))
+    coadd, detection = write_out(coadd, detection)
     return (coadd[None], detection)
 
 

time: 39.6 us -> 34 us (0.86); the launches traced: 39 us -> 33.9 us
  local copies, waits for them, and re-layouts: 2.95 us -> 0 us
  Pallas kernels: 34.7 us -> 32.6 us
    unnamed x2 -> x0, local copies, waits for them, and re-layouts: 2.95 us -> none
    pallas_call x1 -> x2, Pallas kernels: 20.7 us -> 17.9 us  [the longest x1 16.3 us: local_sums(): pl.pallas_call(sums_kernel, out_shape=(jax.ShapeDtypeStruct((tiles, size...]
    pallas_call x1, Pallas kernels: 14 us -> 14.8 us  [owner_coadd(): pl.pallas_call(functools.partial(owner_kernel, owners, bands), out_shape=...]
where the time goes in v3:
time: 34 us; the launch traced here: 33.9 us
  Pallas kernels  32.6 us (96%)
  between operations  1.3 us (4%)
    pallas_call x1, Pallas kernels, local_sums(): pl.pallas_call(sums_kernel, out_shape=(jax.ShapeDtypeStruct((tiles, size...  16.3 us
    pallas_call x1, Pallas kernels, owner_coadd(): pl.pallas_call(functools.partial(owner_kernel, owners, bands), out_shape=...  14.8 us
    pallas_call x1, Pallas kernels, write_out(): pl.pallas_call(write_kernel, out_shape=(out, out), in_specs=[vmem, vmem],...  1.53 us

profile of v3, /device:TPU:0, one launch (start us, length us, event | category | flops | bytes accessed | tf_op | source)
XLA Modules:
  0.0 33.9 jit_solution(1511925911687119428)
XLA Ops:
  1.3 16.3 %local_sums.1 = (bf16[8,160,128]{2,1,0:T(8,128)(2,1)}, f32[8,128]{1,0:T(8,128)}) custom-call(s32[1,192]{1,0:T(1,128)} %bitcast.18, s32[1,192]{1,0:T(1,128)} %visit_hbm.1, f32[1,24]{1,0:T(1,128)} %calib_hbm.1, s32[1,24]{1,0:T(1,128)} %weights_hbm.1, f32[1,1]{1,0:T(1,128)} %bitcast.13.gain_hbm, s32[4,192]{1,0:T(4,128)} %bitcast.16, f32[21,2,192]{2,1,0:T(2,128)} %bitcast.15, ...), custom_call_target="tpu_custom_call" | custom-call | tf_op jit(solution)/shard_map/local_sums/pallas_call | solution.py:255
  17.6 14.8 %owner_coadd.1 = (f32[128,128]{1,0:T(8,128)}, f32[128,128]{1,0:T(8,128)}) custom-call(f32[8,128]{1,0:T(8,128)} %get-tuple-element.8.gain_ref, bf16[8,160,128]{2,1,0:T(8,128)(2,1)} %get-tuple-element.9.sums_ref), custom_call_target="tpu_custom_call" | custom-call | tf_op jit(solution)/shard_map/owner_coadd/pallas_call | solution.py:392
  32.4 1.5 %write_out.1 = (f32[128,128]{1,0:T(8,128)}, f32[128,128]{1,0:T(8,128)}) custom-call(f32[128,128]{1,0:T(8,128)} %get-tuple-element.10.coadd_ref, f32[128,128]{1,0:T(8,128)} %get-tuple-element.11.det_ref), custom_call_target="tpu_custom_call" | custom-call | tf_op jit(solution)/shard_map/write_out/pallas_call | solution.py:429

commit v4 on v3

--- a/solution.py
+++ b/solution.py
@@ -48,22 +48,19 @@
     return first, last
 
 
-def band_matrix(ref, p, size, masks):
-    sub, keep = masks
-    row = [jnp.broadcast_to(ref[v, pl.ds(p, 1), :], (8, size)) for v in range(7)]
-    top = jnp.where(sub == 0, row[0], jnp.where(sub == 1, row[1], jnp.where(sub == 2, row[2], row[3])))
-    end = jnp.where(sub == 7, row[4], jnp.where(sub == 6, row[5], jnp.where(sub == 5, row[6], row[3])))
-    base = pltpu.roll(row[3], 0, 1, stride=1, stride_axis=0)
-    top = pltpu.roll(top, 0, 1, stride=1, stride_axis=0)
-    end = pltpu.roll(end, size - 8, 1, stride=1, stride_axis=0)
+def spread(ref, p, size):
+    return [jnp.broadcast_to(ref[v, pl.ds(p, 1), :], (8, size)) for v in range(7)]
+
+
+def turn(x, shift, size):
+    return pltpu.roll(x, shift % size, 1, stride=1, stride_axis=0)
+
+
+def assemble(base, top, second, before, end, keep, size):
     tiles = size // 8
-    next8 = pltpu.roll(base, 8, 1)
-    head = [jnp.where(keep[0], top, 0.0), jnp.where(keep[1], next8, 0.0)]
-    tail = [
-        jnp.where(keep[tiles - 2], pltpu.roll(base, size - 16, 1), 0.0),
-        jnp.where(keep[tiles - 1], end, 0.0),
-    ]
-    pair = jnp.concatenate([base, next8], axis=0).astype(jnp.bfloat16)
+    head = [jnp.where(keep[0], top, 0.0), jnp.where(keep[1], second, 0.0)]
+    tail = [jnp.where(keep[tiles - 2], before, 0.0), jnp.where(keep[tiles - 1], end, 0.0)]
+    pair = jnp.concatenate([base, pltpu.roll(base, 8, 1)], axis=0).astype(jnp.bfloat16)
     parts = [jnp.concatenate(head, axis=0).astype(jnp.bfloat16)]
     for v in range(1, tiles // 2 - 1):
         parts.append(pltpu.roll(pair, 16 * v, 1))
@@ -71,12 +68,39 @@
     return parts
 
 
+def row_band(ref, p, size, sub, keep):
+    row = spread(ref, p, size)
+    top = jnp.where(sub == 0, row[0], jnp.where(sub == 1, row[1], jnp.where(sub == 2, row[2], row[3])))
+    end = jnp.where(sub == 7, row[4], jnp.where(sub == 6, row[5], jnp.where(sub == 5, row[6], row[3])))
+    base = turn(row[3], 0, size)
+    return assemble(
+        base, turn(top, 0, size), pltpu.roll(base, 8, 1), pltpu.roll(base, size - 16, 1),
+        turn(end, size - 8, size), keep, size,
+    )
+
+
+def column_band(ref, p, size, spots, keep):
+    row = spread(ref, p, size)
+
+    def edged(tile, three):
+        x = row[3]
+        for i in range(3):
+            x = jnp.where(spots[tile, i], row[three + i], x)
+        return turn(x, 8 * tile, size)
+
+    last = size // 8 - 1
+    return assemble(
+        turn(row[3], 0, size), edged(0, 0), edged(1, 0), edged(last - 1, 4), edged(last, 4),
+        keep, size,
+    )
+
+
 def sums_kernel(
-    tile_hbm, visit_hbm, calib_hbm, weights_hbm, gain_hbm, words_hbm, taps_hbm, shifts_hbm, pieces_ref,
+    tile_hbm, visit_hbm, calib_hbm, weights_hbm, gain_ref, words_hbm, taps_hbm, shifts_hbm, pieces_ref,
     out_ref, gain_out,
     pbuf, words_ref, taps_ref, shifts_ref, padded, columns, left_taps, right_taps, good,
     acc, dacc, lbuf, rbuf, ibuf, cbuf,
-    tile_ref, visit_ref, calib_ref, weights_ref, gain_ref, slots, blk_tile, cnt, cur, sems, small_sems,
+    tile_ref, visit_ref, calib_ref, weights_ref, slots, blk_tile, cnt, cur, sems, small_sems,
 ):
     count, size, _ = pieces_ref.shape
     tiles = acc.shape[0]
@@ -88,7 +112,7 @@
             (
                 (tile_hbm, tile_ref), (shifts_hbm, shifts_ref), (taps_hbm, taps_ref),
                 (words_hbm, words_ref), (visit_hbm, visit_ref), (calib_hbm, calib_ref),
-                (weights_hbm, weights_ref), (gain_hbm, gain_ref),
+                (weights_hbm, weights_ref),
             )
         )
     ]
@@ -126,7 +150,7 @@
     for copy in smalls:
         copy.wait()
 
-    gain_out[...] = jnp.full(gain_out.shape, gain_ref[0, 0])
+    gain_out[...] = jnp.full(gain_out.shape, gain_ref[0])
 
     def place(i, used):
         t = tile_ref[0, i]
@@ -152,13 +176,21 @@
     inside = (place_lane < block - reach) | (place_lane >= size - reach)
     for d, table in ((0, left_taps), (1, right_taps)):
         taps = taps_ref[:, d, :]
+        if d == 1:
+            taps = jnp.concatenate(
+                [taps[t : t + 1, :] for t in range(taps_count - 1, -1, -1)], axis=0
+            )
         kernel = taps / jnp.sum(taps, axis=0, keepdims=True)
         kernel = kernel.astype(jnp.bfloat16).astype(jnp.float32)
         padded[d, 2 * SIDE : 2 * SIDE + taps_count, 0:count] = kernel
         shift = jnp.concatenate(
             [shifts_ref[d : d + 1, :], jnp.zeros((1, wide - count), jnp.float32)], axis=1
         )
-        first, last = tap_columns(padded.at[d], shift, block)
+        if d == 0:
+            first, last = tap_columns(padded.at[d], shift, block)
+        else:
+            last, first = tap_columns(padded.at[d], -shift, block)
+            first, last = first + last[3:], last[:3]
         for v, rows in enumerate(first):
             columns[0, block * v : block * (v + 1), :] = rows
         for v, rows in enumerate(last):
@@ -184,7 +216,13 @@
     lane = lax.broadcasted_iota(jnp.int32, (8, size), 1)
     final = size // 8 - 1
     keep = {v: jnp.abs(lane - sub - 8 * v) <= reach for v in (0, 1, final - 1, final)}
-    masks = (sub, keep)
+    spots = {}
+    for tile in (0, 1):
+        for i in range(3):
+            spots[tile, i] = lane == ((i - sub - 8 * tile) & (size - 1))
+    for tile in (final - 1, final):
+        for i in range(3):
+            spots[tile, i] = lane == ((size - 1 - i - sub - 8 * tile) & (size - 1))
 
     def piece_of(step, g):
         return jnp.maximum(slots[step * GROUP + g], 0)
@@ -197,25 +235,21 @@
 
     def build_right(step):
         for g in range(GROUP):
-            p = piece_of(step, g)
-            mask = jnp.broadcast_to(good[pl.ds(p, 1), :], (16, size)).astype(jnp.bfloat16)
-            parts = band_matrix(right_taps, p, size, masks)
+            parts = column_band(right_taps, piece_of(step, g), size, spots, keep)
             for v, part in enumerate(parts):
-                rbuf[g, 16 * v : 16 * v + 16, :] = part * mask
+                rbuf[g, 16 * v : 16 * v + 16, :] = part
 
     def build_left(step):
         for g in range(GROUP):
-            p = piece_of(step, g)
-            parts = band_matrix(left_taps, p, size, masks)
+            parts = row_band(left_taps, piece_of(step, g), size, sub, keep)
             for v, part in enumerate(parts):
                 lbuf[16 * v : 16 * v + 16, g * size : (g + 1) * size] = part
 
     for copy in copies:
         copy.wait()
     build_right(0)
-    ones = jnp.ones((16, size), jnp.bfloat16)
-
-    def step_body(k, carry):
+
+    def add_up(k):
         t = blk_tile[k]
         part = jnp.dot(lbuf[...], ibuf[...], preferred_element_type=jnp.float32)
         acc[t] = acc[t] + part
@@ -227,20 +261,24 @@
             ).astype(jnp.float32)
             den = den + jnp.sum(rim, axis=1, keepdims=True) * cbuf[g, 0:1, :]
         dacc[t] = den
+
+    def step_body(k, carry):
+        add_up(k)
         for g in range(GROUP):
             p = piece_of(k, g)
             w, factor = weight_of(k, g)
-            x = jnp.concatenate([pbuf[p], ones], axis=0)
-            y = lax.dot_general(
-                x, rbuf[g], (((1,), (1,)), ((), ())), preferred_element_type=jnp.float32
-            )
+            mask = jnp.broadcast_to(good[pl.ds(p, 1), :], (16, size)).astype(jnp.bfloat16)
+            rows = [pbuf[p, 16 * v : 16 * v + 16, :] * mask for v in range(size // 16)]
+            x = jnp.concatenate(rows + [mask], axis=0)
+            y = jnp.dot(x, rbuf[g], preferred_element_type=jnp.float32)
             ibuf[g * size : (g + 1) * size, :] = (y[0:size] * factor).astype(jnp.bfloat16)
             cbuf[g] = y[size : size + 8] * w
         build_left(k)
         build_right(k + 1)
         return carry
 
-    lax.fori_loop(0, used + 1, step_body, 0)
+    lax.fori_loop(0, used, step_body, 0)
+    add_up(used)
     for t in range(tiles):
         out_ref[t, 0:size, :] = acc[t].astype(jnp.bfloat16)
         out_ref[t, size : size + 2 * EDGE, :] = dacc[t].astype(jnp.bfloat16)
@@ -258,7 +296,7 @@
             jax.ShapeDtypeStruct((tiles, size + 2 * EDGE, size), jnp.bfloat16),
             jax.ShapeDtypeStruct((8, size), jnp.float32),
         ),
-        in_specs=[hbm] * 9,
+        in_specs=[hbm] * 4 + [pl.BlockSpec(memory_space=pltpu.SMEM)] + [hbm] * 4,
         out_specs=(pl.BlockSpec(memory_space=pltpu.VMEM),) * 2,
         scratch_shapes=[
             pltpu.VMEM((count, size, size), jnp.bfloat16),
@@ -280,13 +318,12 @@
             pltpu.SMEM(visit.shape, jnp.int32),
             pltpu.SMEM(calib.shape, jnp.float32),
             pltpu.SMEM(weights.shape, jnp.int32),
-            pltpu.SMEM(gain.shape, jnp.float32),
             pltpu.SMEM((blocks * GROUP,), jnp.int32),
             pltpu.SMEM((blocks + 1,), jnp.int32),
             pltpu.SMEM((tiles,), jnp.int32),
             pltpu.SMEM((tiles,), jnp.int32),
             pltpu.SemaphoreType.DMA((chunks,)),
-            pltpu.SemaphoreType.DMA((8,)),
+            pltpu.SemaphoreType.DMA((7,)),
         ],
         compiler_params=pltpu.CompilerParams(vmem_limit_bytes=56 * 1024 * 1024),
         name="local_sums",
@@ -418,19 +455,26 @@
     )(gain, sums)
 
 
-def write_kernel(coadd_ref, det_ref, coadd_out, det_out):
-    coadd_out[...] = coadd_ref[...]
-    det_out[...] = det_ref[...]
+def write_kernel(coadd_ref, det_ref, coadd_out, det_out, sems):
+    copies = [
+        pltpu.make_async_copy(coadd_ref, coadd_out, sems.at[0]),
+        pltpu.make_async_copy(det_ref, det_out, sems.at[1]),
+    ]
+    for copy in copies:
+        copy.start()
+    for copy in copies:
+        copy.wait()
 
 
 def write_out(coadd, detection):
-    vmem = pl.BlockSpec(memory_space=pltpu.VMEM)
+    hbm = pl.BlockSpec(memory_space=pltpu.HBM)
     out = jax.ShapeDtypeStruct(coadd.shape, coadd.dtype)
     return pl.pallas_call(
         write_kernel,
         out_shape=(out, out),
-        in_specs=[vmem, vmem],
-        out_specs=(vmem, vmem),
+        in_specs=[hbm, hbm],
+        out_specs=(hbm, hbm),
+        scratch_shapes=[pltpu.SemaphoreType.DMA((2,))],
         compiler_params=pltpu.CompilerParams(vmem_limit_bytes=56 * 1024 * 1024),
         name="write_out",
     )(coadd, detection)
@@ -440,7 +484,7 @@
     owners = lax.axis_size("vis")
     sums, gain = local_sums(
         pieces[0], visit, tile_map[:, :, 0], good_columns[0].T, psf_taps[0].transpose(2, 1, 0),
-        shifts[0].T, calib, weights, band_gain.reshape(1, 1), owners,
+        shifts[0].T, calib, weights, band_gain, owners,
     )
     coadd, detection = owner_coadd(gain, sums, owners, lax.axis_size("band"))
     coadd, detection = write_out(coadd, detection)

time: 34 us -> 37.4 us (1.100)
  Pallas kernels: 32.6 us -> 36.1 us
    pallas_call x1, Pallas kernels: 1.53 us -> 5.09 us  [write_out(): pl.pallas_call(write_kernel, out_shape=(out, out), in_specs=[hbm, hbm], o...]
    pallas_call x1, Pallas kernels: 16.3 us -> 15.5 us  [local_sums(): pl.pallas_call(sums_kernel, out_shape=(jax.ShapeDtypeStruct((tiles, size...]
    pallas_call x1, Pallas kernels: 14.8 us -> 15.5 us  [owner_coadd(): pl.pallas_call(functools.partial(owner_kernel, owners, bands), out_shape=...]
where the time goes in v4:
time: 37.4 us
  Pallas kernels  36.1 us (97%)
  between operations  1.3 us (3%)
    pallas_call x1, Pallas kernels, local_sums(): pl.pallas_call(sums_kernel, out_shape=(jax.ShapeDtypeStruct((tiles, size...  15.5 us
    pallas_call x1, Pallas kernels, owner_coadd(): pl.pallas_call(functools.partial(owner_kernel, owners, bands), out_shape=...  15.5 us
    pallas_call x1, Pallas kernels, write_out(): pl.pallas_call(write_kernel, out_shape=(out, out), in_specs=[hbm, hbm], o...  5.09 us

profile of v4, /device:TPU:0, one launch (start us, length us, event | category | flops | bytes accessed | tf_op | source)
XLA Modules:
  0.0 37.4 jit_solution(2285622327399168448)
XLA Ops:
  1.3 15.5 %local_sums.1 = (bf16[8,160,128]{2,1,0:T(8,128)(2,1)}, f32[8,128]{1,0:T(8,128)}) custom-call(s32[1,192]{1,0:T(1,128)} %bitcast.16, s32[1,192]{1,0:T(1,128)} %visit_hbm.1, f32[1,24]{1,0:T(1,128)} %calib_hbm.1, s32[1,24]{1,0:T(1,128)} %weights_hbm.1, f32[1]{0:T(128)S(6)} %copy.11.gain_ref, s32[4,192]{1,0:T(4,128)} %bitcast.14, f32[21,2,192]{2,1,0:T(2,128)} %bitcast.13, ...), custom_call_target="tpu_custom_call" | custom-call | tf_op jit(solution)/shard_map/local_sums/pallas_call | solution.py:293
  16.8 15.5 %owner_coadd.1 = (f32[128,128]{1,0:T(8,128)}, f32[128,128]{1,0:T(8,128)}) custom-call(f32[8,128]{1,0:T(8,128)} %get-tuple-element.8.gain_ref, bf16[8,160,128]{2,1,0:T(8,128)(2,1)} %get-tuple-element.9.sums_ref), custom_call_target="tpu_custom_call" | custom-call | tf_op jit(solution)/shard_map/owner_coadd/pallas_call | solution.py:429
  32.3 5.1 %write_out.1 = (f32[128,128]{1,0:T(8,128)}, f32[128,128]{1,0:T(8,128)}) custom-call(f32[128,128]{1,0:T(8,128)} %get-tuple-element.10.coadd_ref, f32[128,128]{1,0:T(8,128)} %get-tuple-element.11.det_ref), custom_call_target="tpu_custom_call" | custom-call | tf_op jit(solution)/shard_map/write_out/pallas_call | solution.py:472

commit v5 on v4

--- a/solution.py
+++ b/solution.py
@@ -233,21 +233,20 @@
         w = jnp.where(p >= 0, weights_ref[0, v], 0).astype(jnp.float32)
         return w, w * calib_ref[0, v]
 
-    def build_right(step):
-        for g in range(GROUP):
-            parts = column_band(right_taps, piece_of(step, g), size, spots, keep)
-            for v, part in enumerate(parts):
-                rbuf[g, 16 * v : 16 * v + 16, :] = part
-
-    def build_left(step):
-        for g in range(GROUP):
-            parts = row_band(left_taps, piece_of(step, g), size, sub, keep)
-            for v, part in enumerate(parts):
-                lbuf[16 * v : 16 * v + 16, g * size : (g + 1) * size] = part
-
+    def build_right(step, g):
+        parts = column_band(right_taps, piece_of(step, g), size, spots, keep)
+        for v, part in enumerate(parts):
+            rbuf[g, 16 * v : 16 * v + 16, :] = part
+
+    def build_left(step, g):
+        parts = row_band(left_taps, piece_of(step, g), size, sub, keep)
+        for v, part in enumerate(parts):
+            lbuf[16 * v : 16 * v + 16, g * size : (g + 1) * size] = part
+
+    for g in range(GROUP):
+        build_right(0, g)
     for copy in copies:
         copy.wait()
-    build_right(0)
 
     def add_up(k):
         t = blk_tile[k]
@@ -273,8 +272,8 @@
             y = jnp.dot(x, rbuf[g], preferred_element_type=jnp.float32)
             ibuf[g * size : (g + 1) * size, :] = (y[0:size] * factor).astype(jnp.bfloat16)
             cbuf[g] = y[size : size + 8] * w
-        build_left(k)
-        build_right(k + 1)
+            build_left(k, g)
+            build_right(k + 1, g)
         return carry
 
     lax.fori_loop(0, used, step_body, 0)
@@ -455,26 +454,19 @@
     )(gain, sums)
 
 
-def write_kernel(coadd_ref, det_ref, coadd_out, det_out, sems):
-    copies = [
-        pltpu.make_async_copy(coadd_ref, coadd_out, sems.at[0]),
-        pltpu.make_async_copy(det_ref, det_out, sems.at[1]),
-    ]
-    for copy in copies:
-        copy.start()
-    for copy in copies:
-        copy.wait()
+def write_kernel(coadd_ref, det_ref, coadd_out, det_out):
+    coadd_out[...] = coadd_ref[...]
+    det_out[...] = det_ref[...]
 
 
 def write_out(coadd, detection):
-    hbm = pl.BlockSpec(memory_space=pltpu.HBM)
+    vmem = pl.BlockSpec(memory_space=pltpu.VMEM)
     out = jax.ShapeDtypeStruct(coadd.shape, coadd.dtype)
     return pl.pallas_call(
         write_kernel,
         out_shape=(out, out),
-        in_specs=[hbm, hbm],
-        out_specs=(hbm, hbm),
-        scratch_shapes=[pltpu.SemaphoreType.DMA((2,))],
+        in_specs=[vmem, vmem],
+        out_specs=(vmem, vmem),
         compiler_params=pltpu.CompilerParams(vmem_limit_bytes=56 * 1024 * 1024),
         name="write_out",
     )(coadd, detection)

time: 37.4 us -> 34.1 us (0.912); the launches traced: 37.4 us -> 33.7 us
  Pallas kernels: 36.1 us -> 32.4 us
    pallas_call x1, Pallas kernels: 5.09 us -> 1.53 us  [write_out(): pl.pallas_call(write_kernel, out_shape=(out, out), in_specs=[vmem, vmem],...]
    pallas_call x1, Pallas kernels: 15.5 us -> 14.5 us  [owner_coadd(): pl.pallas_call(functools.partial(owner_kernel, owners, bands), out_shape=...]
    pallas_call x1, Pallas kernels: 15.5 us -> 16.4 us  [local_sums(): pl.pallas_call(sums_kernel, out_shape=(jax.ShapeDtypeStruct((tiles, size...]
where the time goes in v5:
time: 34.1 us; the launch traced here: 33.7 us
  Pallas kernels  32.4 us (95%)
  between operations  1.3 us (4%)
    pallas_call x1, Pallas kernels, local_sums(): pl.pallas_call(sums_kernel, out_shape=(jax.ShapeDtypeStruct((tiles, size...  16.4 us
    pallas_call x1, Pallas kernels, owner_coadd(): pl.pallas_call(functools.partial(owner_kernel, owners, bands), out_shape=...  14.5 us
    pallas_call x1, Pallas kernels, write_out(): pl.pallas_call(write_kernel, out_shape=(out, out), in_specs=[vmem, vmem],...  1.53 us

profile of v5, /device:TPU:0, one launch (start us, length us, event | category | flops | bytes accessed | tf_op | source)
XLA Modules:
  0.0 33.7 jit_solution(10963655334798457746)
XLA Ops:
  1.3 16.4 %local_sums.1 = (bf16[8,160,128]{2,1,0:T(8,128)(2,1)}, f32[8,128]{1,0:T(8,128)}) custom-call(s32[1,192]{1,0:T(1,128)} %bitcast.16, s32[1,192]{1,0:T(1,128)} %visit_hbm.1, f32[1,24]{1,0:T(1,128)} %calib_hbm.1, s32[1,24]{1,0:T(1,128)} %weights_hbm.1, f32[1]{0:T(128)S(6)} %copy.11.gain_ref, s32[4,192]{1,0:T(4,128)} %bitcast.14, f32[21,2,192]{2,1,0:T(2,128)} %bitcast.13, ...), custom_call_target="tpu_custom_call" | custom-call | tf_op jit(solution)/shard_map/local_sums/pallas_call | solution.py:292
  17.7 14.5 %owner_coadd.1 = (f32[128,128]{1,0:T(8,128)}, f32[128,128]{1,0:T(8,128)}) custom-call(f32[8,128]{1,0:T(8,128)} %get-tuple-element.8.gain_ref, bf16[8,160,128]{2,1,0:T(8,128)(2,1)} %get-tuple-element.9.sums_ref), custom_call_target="tpu_custom_call" | custom-call | tf_op jit(solution)/shard_map/owner_coadd/pallas_call | solution.py:428
  32.2 1.5 %write_out.1 = (f32[128,128]{1,0:T(8,128)}, f32[128,128]{1,0:T(8,128)}) custom-call(f32[128,128]{1,0:T(8,128)} %get-tuple-element.10.coadd_ref, f32[128,128]{1,0:T(8,128)} %get-tuple-element.11.det_ref), custom_call_target="tpu_custom_call" | custom-call | tf_op jit(solution)/shard_map/write_out/pallas_call | solution.py:465

commit v6 on v5

--- a/solution.py
+++ b/solution.py
@@ -8,7 +8,9 @@
 from jax.experimental.pallas import tpu as pltpu
 from jax.sharding import PartitionSpec as P
 
-GROUP = 8
+GROUP = 4
+BLOCKS = 2
+STEP = GROUP * BLOCKS
 SIDE = 3
 EDGE = 16
 MESH = pl.DeviceIdType.MESH
@@ -159,7 +161,7 @@
         fresh = inside == 0
         b = jnp.where(fresh, used, cur[t])
         cur[t] = b
-        blk_tile[b + 1] = t
+        blk_tile[b + BLOCKS] = t
         slots[b * GROUP + inside] = i
         cnt[t] = n + 1
         return jnp.where(fresh, used + 1, used)
@@ -225,10 +227,10 @@
             spots[tile, i] = lane == ((size - 1 - i - sub - 8 * tile) & (size - 1))
 
     def piece_of(step, g):
-        return jnp.maximum(slots[step * GROUP + g], 0)
+        return jnp.maximum(slots[step * STEP + g], 0)
 
     def weight_of(step, g):
-        p = slots[step * GROUP + g]
+        p = slots[step * STEP + g]
         v = visit_ref[0, jnp.maximum(p, 0)]
         w = jnp.where(p >= 0, weights_ref[0, v], 0).astype(jnp.float32)
         return w, w * calib_ref[0, v]
@@ -243,27 +245,29 @@
         for v, part in enumerate(parts):
             lbuf[16 * v : 16 * v + 16, g * size : (g + 1) * size] = part
 
-    for g in range(GROUP):
+    for g in range(STEP):
         build_right(0, g)
     for copy in copies:
         copy.wait()
 
     def add_up(k):
-        t = blk_tile[k]
-        part = jnp.dot(lbuf[...], ibuf[...], preferred_element_type=jnp.float32)
-        acc[t] = acc[t] + part
-        den = dacc[t]
-        for g in range(GROUP):
-            cols = slice(g * size, (g + 1) * size)
-            rim = jnp.concatenate(
-                [lbuf[0:EDGE, cols], lbuf[size - EDGE : size, cols]], axis=0
-            ).astype(jnp.float32)
-            den = den + jnp.sum(rim, axis=1, keepdims=True) * cbuf[g, 0:1, :]
-        dacc[t] = den
+        for j in range(BLOCKS):
+            t = blk_tile[k * BLOCKS + j]
+            here = slice(j * GROUP * size, (j + 1) * GROUP * size)
+            part = jnp.dot(lbuf[:, here], ibuf[here, :], preferred_element_type=jnp.float32)
+            acc[t] = acc[t] + part
+            den = dacc[t]
+            for g in range(j * GROUP, (j + 1) * GROUP):
+                cols = slice(g * size, (g + 1) * size)
+                rim = jnp.concatenate(
+                    [lbuf[0:EDGE, cols], lbuf[size - EDGE : size, cols]], axis=0
+                ).astype(jnp.float32)
+                den = den + jnp.sum(rim, axis=1, keepdims=True) * cbuf[g, 0:1, :]
+            dacc[t] = den
 
     def step_body(k, carry):
         add_up(k)
-        for g in range(GROUP):
+        for g in range(STEP):
             p = piece_of(k, g)
             w, factor = weight_of(k, g)
             mask = jnp.broadcast_to(good[pl.ds(p, 1), :], (16, size)).astype(jnp.bfloat16)
@@ -276,8 +280,9 @@
             build_right(k + 1, g)
         return carry
 
-    lax.fori_loop(0, used, step_body, 0)
-    add_up(used)
+    steps = (used + (BLOCKS - 1)) // BLOCKS
+    lax.fori_loop(0, steps, step_body, 0)
+    add_up(steps)
     for t in range(tiles):
         out_ref[t, 0:size, :] = acc[t].astype(jnp.bfloat16)
         out_ref[t, size : size + 2 * EDGE, :] = dacc[t].astype(jnp.bfloat16)
@@ -285,7 +290,8 @@
 
 def local_sums(pieces, visit, tile, words, taps, shifts, calib, weights, gain, tiles):
     count, size, _ = pieces.shape
-    blocks = (count + tiles * (GROUP - 1)) // GROUP + 2
+    blocks = (count + tiles * (GROUP - 1)) // GROUP
+    blocks = (-(-blocks // BLOCKS) + 2) * BLOCKS
     hbm = pl.BlockSpec(memory_space=pltpu.HBM)
     chunks = 8 if count % 8 == 0 else 1
     wide = -(-count // size) * size
@@ -309,16 +315,16 @@
             pltpu.VMEM((wide, size), jnp.float32),
             pltpu.VMEM((tiles, size, size), jnp.float32),
             pltpu.VMEM((tiles, 2 * EDGE, size), jnp.float32),
-            pltpu.VMEM((size, GROUP * size), jnp.bfloat16),
-            pltpu.VMEM((GROUP, size, size), jnp.bfloat16),
-            pltpu.VMEM((GROUP * size, size), jnp.bfloat16),
-            pltpu.VMEM((GROUP, 8, size), jnp.float32),
+            pltpu.VMEM((size, STEP * size), jnp.bfloat16),
+            pltpu.VMEM((STEP, size, size), jnp.bfloat16),
+            pltpu.VMEM((STEP * size, size), jnp.bfloat16),
+            pltpu.VMEM((STEP, 8, size), jnp.float32),
             pltpu.SMEM(tile.shape, jnp.int32),
             pltpu.SMEM(visit.shape, jnp.int32),
             pltpu.SMEM(calib.shape, jnp.float32),
             pltpu.SMEM(weights.shape, jnp.int32),
             pltpu.SMEM((blocks * GROUP,), jnp.int32),
-            pltpu.SMEM((blocks + 1,), jnp.int32),
+            pltpu.SMEM((blocks + BLOCKS,), jnp.int32),
             pltpu.SMEM((tiles,), jnp.int32),
             pltpu.SMEM((tiles,), jnp.int32),
             pltpu.SemaphoreType.DMA((chunks,)),

time: 34.1 us -> 33.5 us (0.982); the launches traced: 33.7 us -> 33.5 us
    pallas_call x1, Pallas kernels: 16.4 us -> 15.2 us  [local_sums(): pl.pallas_call(sums_kernel, out_shape=(jax.ShapeDtypeStruct((tiles, size...]
    pallas_call x1, Pallas kernels: 14.5 us -> 15.4 us  [owner_coadd(): pl.pallas_call(functools.partial(owner_kernel, owners, bands), out_shape=...]
where the time goes in v6:
time: 33.5 us
  Pallas kernels  32.2 us (96%)
  between operations  1.3 us (4%)
    pallas_call x1, Pallas kernels, owner_coadd(): pl.pallas_call(functools.partial(owner_kernel, owners, bands), out_shape=...  15.4 us
    pallas_call x1, Pallas kernels, local_sums(): pl.pallas_call(sums_kernel, out_shape=(jax.ShapeDtypeStruct((tiles, size...  15.2 us
    pallas_call x1, Pallas kernels, write_out(): pl.pallas_call(write_kernel, out_shape=(out, out), in_specs=[vmem, vmem],...  1.53 us

profile of v6, /device:TPU:0, one launch (start us, length us, event | category | flops | bytes accessed | tf_op | source)
XLA Modules:
  0.0 33.5 jit_solution(8376888314443784648)
XLA Ops:
  1.3 15.2 %local_sums.1 = (bf16[8,160,128]{2,1,0:T(8,128)(2,1)}, f32[8,128]{1,0:T(8,128)}) custom-call(s32[1,192]{1,0:T(1,128)} %bitcast.16, s32[1,192]{1,0:T(1,128)} %visit_hbm.1, f32[1,24]{1,0:T(1,128)} %calib_hbm.1, s32[1,24]{1,0:T(1,128)} %weights_hbm.1, f32[1]{0:T(128)S(6)} %copy.11.gain_ref, s32[4,192]{1,0:T(4,128)} %bitcast.14, f32[21,2,192]{2,1,0:T(2,128)} %bitcast.13, ...), custom_call_target="tpu_custom_call" | custom-call | tf_op jit(solution)/shard_map/local_sums/pallas_call | solution.py:298
  16.5 15.4 %owner_coadd.1 = (f32[128,128]{1,0:T(8,128)}, f32[128,128]{1,0:T(8,128)}) custom-call(f32[8,128]{1,0:T(8,128)} %get-tuple-element.8.gain_ref, bf16[8,160,128]{2,1,0:T(8,128)(2,1)} %get-tuple-element.9.sums_ref), custom_call_target="tpu_custom_call" | custom-call | tf_op jit(solution)/shard_map/owner_coadd/pallas_call | solution.py:434
  31.9 1.5 %write_out.1 = (f32[128,128]{1,0:T(8,128)}, f32[128,128]{1,0:T(8,128)}) custom-call(f32[128,128]{1,0:T(8,128)} %get-tuple-element.10.coadd_ref, f32[128,128]{1,0:T(8,128)} %get-tuple-element.11.det_ref), custom_call_target="tpu_custom_call" | custom-call | tf_op jit(solution)/shard_map/write_out/pallas_call | solution.py:471

commit v7 on v6

--- a/solution.py
+++ b/solution.py
@@ -147,6 +147,7 @@
         dacc[t] = jnp.zeros((2 * EDGE, size), jnp.float32)
     lbuf[...] = jnp.zeros_like(lbuf)
     ibuf[...] = jnp.zeros_like(ibuf)
+    rbuf[...] = jnp.zeros_like(rbuf)
     cbuf[...] = jnp.zeros_like(cbuf)
     padded[...] = jnp.zeros_like(padded)
     for copy in smalls:
@@ -238,7 +239,8 @@
     def build_right(step, g):
         parts = column_band(right_taps, piece_of(step, g), size, spots, keep)
         for v, part in enumerate(parts):
-            rbuf[g, 16 * v : 16 * v + 16, :] = part
+            here = size * (g % 2)
+            rbuf[g // 2, here + 16 * v : here + 16 * v + 16, here : here + size] = part
 
     def build_left(step, g):
         parts = row_band(left_taps, piece_of(step, g), size, sub, keep)
@@ -267,17 +269,22 @@
 
     def step_body(k, carry):
         add_up(k)
-        for g in range(STEP):
-            p = piece_of(k, g)
-            w, factor = weight_of(k, g)
-            mask = jnp.broadcast_to(good[pl.ds(p, 1), :], (16, size)).astype(jnp.bfloat16)
-            rows = [pbuf[p, 16 * v : 16 * v + 16, :] * mask for v in range(size // 16)]
-            x = jnp.concatenate(rows + [mask], axis=0)
-            y = jnp.dot(x, rbuf[g], preferred_element_type=jnp.float32)
-            ibuf[g * size : (g + 1) * size, :] = (y[0:size] * factor).astype(jnp.bfloat16)
-            cbuf[g] = y[size : size + 8] * w
-            build_left(k, g)
-            build_right(k + 1, g)
+        for first in range(0, STEP, 2):
+            sides = []
+            for g in (first, first + 1):
+                p = piece_of(k, g)
+                mask = jnp.broadcast_to(good[pl.ds(p, 1), :], (16, size)).astype(jnp.bfloat16)
+                rows = [pbuf[p, 16 * v : 16 * v + 16, :] * mask for v in range(size // 16)]
+                sides.append(jnp.concatenate(rows + [mask], axis=0))
+            x = jnp.concatenate(sides, axis=1)
+            both = jnp.dot(x, rbuf[first // 2], preferred_element_type=jnp.float32)
+            for g in (first, first + 1):
+                w, factor = weight_of(k, g)
+                y = both[:, size * (g - first) : size * (g - first + 1)]
+                ibuf[g * size : (g + 1) * size, :] = (y[0:size] * factor).astype(jnp.bfloat16)
+                cbuf[g] = y[size : size + 8] * w
+                build_left(k, g)
+                build_right(k + 1, g)
         return carry
 
     steps = (used + (BLOCKS - 1)) // BLOCKS
@@ -316,7 +323,7 @@
             pltpu.VMEM((tiles, size, size), jnp.float32),
             pltpu.VMEM((tiles, 2 * EDGE, size), jnp.float32),
             pltpu.VMEM((size, STEP * size), jnp.bfloat16),
-            pltpu.VMEM((STEP, size, size), jnp.bfloat16),
+            pltpu.VMEM((STEP // 2, 2 * size, 2 * size), jnp.bfloat16),
             pltpu.VMEM((STEP * size, size), jnp.bfloat16),
             pltpu.VMEM((STEP, 8, size), jnp.float32),
             pltpu.SMEM(tile.shape, jnp.int32),

time: 33.5 us -> 33.6 us (level)
    pallas_call x1, Pallas kernels: 15.2 us -> 16 us  [local_sums(): pl.pallas_call(sums_kernel, out_shape=(jax.ShapeDtypeStruct((tiles, size...]
    pallas_call x1, Pallas kernels: 15.4 us -> 14.8 us  [owner_coadd(): pl.pallas_call(functools.partial(owner_kernel, owners, bands), out_shape=...]
where the time goes in v7:
time: 33.6 us
  Pallas kernels  32.3 us (96%)
  between operations  1.3 us (4%)
    pallas_call x1, Pallas kernels, local_sums(): pl.pallas_call(sums_kernel, out_shape=(jax.ShapeDtypeStruct((tiles, size...  16 us
    pallas_call x1, Pallas kernels, owner_coadd(): pl.pallas_call(functools.partial(owner_kernel, owners, bands), out_shape=...  14.8 us
    pallas_call x1, Pallas kernels, write_out(): pl.pallas_call(write_kernel, out_shape=(out, out), in_specs=[vmem, vmem],...  1.53 us

profile of v7, /device:TPU:0, one launch (start us, length us, event | category | flops | bytes accessed | tf_op | source)
XLA Modules:
  0.0 33.6 jit_solution(5043190726974886943)
XLA Ops:
  1.3 16.0 %local_sums.1 = (bf16[8,160,128]{2,1,0:T(8,128)(2,1)}, f32[8,128]{1,0:T(8,128)}) custom-call(s32[1,192]{1,0:T(1,128)} %bitcast.16, s32[1,192]{1,0:T(1,128)} %visit_hbm.1, f32[1,24]{1,0:T(1,128)} %calib_hbm.1, s32[1,24]{1,0:T(1,128)} %weights_hbm.1, f32[1]{0:T(128)S(6)} %copy.11.gain_ref, s32[4,192]{1,0:T(4,128)} %bitcast.14, f32[21,2,192]{2,1,0:T(2,128)} %bitcast.13, ...), custom_call_target="tpu_custom_call" | custom-call | tf_op jit(solution)/shard_map/local_sums/pallas_call | solution.py:305
  17.3 14.8 %owner_coadd.1 = (f32[128,128]{1,0:T(8,128)}, f32[128,128]{1,0:T(8,128)}) custom-call(f32[8,128]{1,0:T(8,128)} %get-tuple-element.8.gain_ref, bf16[8,160,128]{2,1,0:T(8,128)(2,1)} %get-tuple-element.9.sums_ref), custom_call_target="tpu_custom_call" | custom-call | tf_op jit(solution)/shard_map/owner_coadd/pallas_call | solution.py:441
  32.0 1.5 %write_out.1 = (f32[128,128]{1,0:T(8,128)}, f32[128,128]{1,0:T(8,128)}) custom-call(f32[128,128]{1,0:T(8,128)} %get-tuple-element.10.coadd_ref, f32[128,128]{1,0:T(8,128)} %get-tuple-element.11.det_ref), custom_call_target="tpu_custom_call" | custom-call | tf_op jit(solution)/shard_map/write_out/pallas_call | solution.py:478
